TPU v7x, 32 devices: a whole 2x2x4 slice. The times are simulated.
32 devices in a mesh: dp: 16 (over z, y, core), patch: 2 (over x).
Axes of the slice: x: 2, y: 2, z: 4, core: 2. Of those that a mesh axis runs over, the one named last changes fastest.
Arguments:
- hidden: bfloat16 [64, 256, 768], P(('dp', 'patch')), may hold values from -6 to 6
- lengths: int32 [64, 4], P(('dp', 'patch')), may hold values from 1 to 64, 128 in all within a row
- image_order: int32 [64, 4], P(('dp', 'patch')), may hold values from 0 to 3, each once within a row
- features: bfloat16 [64, 4, 264, 1408], P('dp', None, 'patch'), may hold values from -6 to 6
- cotangent: bfloat16 [64, 256, 768], P(('dp', 'patch')), may hold values from -6 to 6
- self_weight: bfloat16 [768, 2304], replicated, may hold values from -0.21875 to 0.21875
- output_weight: bfloat16 [768, 768], replicated, may hold values from -0.875 to 0.875
- self_bias: float32 [3, 768], replicated, may hold values from -2 to 2
- norm_gain: float32 [4, 768], replicated, may hold values from 0.5 to 1.5
- norm_shift: float32 [4, 768], replicated, may hold values from -2 to 2
- query_weight: bfloat16 [768, 768], replicated, may hold values from -0.21875 to 0.21875
- image_weight: bfloat16 [1408, 1536], replicated, may hold values from -0.15625 to 0.15625
- cross_weight: bfloat16 [768, 768], replicated, may hold values from -1.75 to 1.75
- cross_bias: float32 [3, 768], replicated, may hold values from -2 to 2
- expand_weight: bfloat16 [768, 6144], replicated, may hold values from -0.21875 to 0.21875
- expand_bias: float32 [6144], replicated, may hold values from -2 to 2
- reduce_weight: bfloat16 [6144, 768], replicated, may hold values from -0.109375 to 0.109375
- reduce_bias: float32 [2, 768], replicated, may hold values from -2 to 2
Outputs:
- mixed: bfloat16 [64, 256, 768], P(('dp', 'patch'))
- hidden_gradient: bfloat16 [64, 256, 768], P(('dp', 'patch'))
- self_weight_gradient: float32 [768, 2304], P('dp', 'patch')
- output_weight_gradient: float32 [768, 768], P('dp', 'patch')
- self_bias_gradient: float32 [3, 768], replicated
- norm_gain_gradient: float32 [4, 768], replicated
- norm_shift_gradient: float32 [4, 768], replicated
- query_weight_gradient: float32 [768, 768], P('dp', 'patch')
- image_weight_gradient: float32 [1408, 1536], P('dp', 'patch')
- cross_weight_gradient: float32 [768, 768], P('dp', 'patch')
- cross_bias_gradient: float32 [3, 768], replicated
- expand_weight_gradient: float32 [768, 6144], P('dp', 'patch')
- expand_bias_gradient: float32 [6144], replicated
- reduce_weight_gradient: float32 [6144, 768], P('dp', 'patch')
- reduce_bias_gradient: float32 [2, 768], replicated
Inputs may be any that keep to these rules, and one draw needn't show every extreme that they name: `lengths`: the 4 captions of a row together fill its 128 caption tokens, and the longest caption of every row has exactly 64 tokens. `image_order`: each row names each of its 4 images once.
All inputs are finite; a program needn't handle non-finite values.
Results may differ from a plain program's by a relative error of at most 0.025.
Values may be sent and summed in bfloat16 or wider, within the bound.
A program may use at most 320 MiB of HBM per device.

v0:
```python
import jax
import jax.numpy as jnp
from jax import lax
from jax.sharding import PartitionSpec as P

HEADS = 12
QUERIES = 32
GROUPS = 4
TEXT = 128
PATCHES = 264
PAD = 7


epsilon = 1e-06
masked_score = -1000000000.0


def product(left, right):
    return jnp.dot(left, right, preferred_element_type=jnp.float32)


def weight_gradient(inputs, slopes):
    return lax.dot_general(
        inputs, slopes, (((0,), (0,)), ((), ())), preferred_element_type=jnp.float32
    )


def input_gradient(slopes, weight):
    return lax.dot_general(
        slopes, weight, (((1,), (1,)), ((), ())), preferred_element_type=jnp.float32
    )


def norm_forward(hidden, scales, shifts):
    row_mean = jnp.mean(hidden, axis=-1, keepdims=True)
    centered = hidden - row_mean
    inverse = lax.rsqrt(jnp.mean(centered * centered, axis=-1, keepdims=True) + epsilon)
    normed = centered * inverse
    return (normed * scales + shifts, normed, inverse)


def norm_backward(slopes, normed, inverse, scales):
    scaled = slopes * scales
    across = (
        scaled
        - jnp.mean(scaled, axis=-1, keepdims=True)
        - normed * jnp.mean(scaled * normed, axis=-1, keepdims=True)
    )
    return (inverse * across, jnp.sum(slopes * normed, axis=0), jnp.sum(slopes, axis=0))


def gelu_slope(preact):
    return (
        0.5 * (1.0 + jax.scipy.special.erf(preact * 0.7071067811865476))
        + preact * jnp.exp(-0.5 * preact * preact) * 0.3989422804014327
    )


def segments(lengths):
    group_ends = jnp.cumsum(lengths, axis=-1, dtype=jnp.int32)
    text_place = jnp.arange(TEXT, dtype=jnp.int32)
    text_group = jnp.sum(
        (group_ends[:, None, :] <= text_place[None, :, None]).astype(jnp.int32),
        axis=-1,
        dtype=jnp.int32,
    )
    query_group = jnp.arange(GROUPS * QUERIES, dtype=jnp.int32) // QUERIES
    query_group = jnp.broadcast_to(query_group[None, :], (lengths.shape[0], GROUPS * QUERIES))
    return jnp.concatenate([query_group, text_group], axis=1)


def split_heads(tensor, head_count):
    return tensor.reshape(tensor.shape[:-1] + (head_count, tensor.shape[-1] // head_count))


def cross_scores(by_image, key_heads, patch_valid, score_scale):
    raw_scores = jnp.einsum(
        "nmqhd,nmphd->nmhqp",
        split_heads(by_image, key_heads.shape[-2]),
        key_heads,
        preferred_element_type=jnp.float32,
    )
    return jnp.where(patch_valid, raw_scores * score_scale, masked_score)


def score_slopes(
    image_probs, prob_slopes, image_delta, by_image, image_kv, image_slope, score_scale
):
    head_count = image_kv.shape[-2]
    score_low = (image_probs * (prob_slopes - image_delta) * score_scale).astype(jnp.bfloat16)
    query_heads = split_heads(by_image, head_count)
    slope_heads = split_heads(image_slope, head_count)
    query_slope = jnp.einsum(
        "nmhqp,nmphd->nmqhd", score_low, image_kv[:, :, :, 0], preferred_element_type=jnp.float32
    )
    key_slope = jnp.einsum(
        "nmhqp,nmqhd->nmphd", score_low, query_heads, preferred_element_type=jnp.float32
    )
    value_slope = jnp.einsum(
        "nmhqp,nmqhd->nmphd",
        image_probs.astype(jnp.bfloat16),
        slope_heads,
        preferred_element_type=jnp.float32,
    )
    paired = jnp.stack([key_slope, value_slope], axis=3).astype(jnp.bfloat16)
    return (
        query_slope.reshape(by_image.shape),
        paired.reshape(-1, 2 * by_image.shape[-1]),
        jnp.sum(value_slope, axis=(0, 1, 2)).reshape(-1),
    )


def local(
    hidden,
    lengths,
    image_order,
    features,
    cotangent,
    self_weight,
    output_weight,
    self_bias,
    norm_gain,
    norm_shift,
    query_weight,
    image_weight,
    cross_weight,
    cross_bias,
    expand_weight,
    expand_bias,
    reduce_weight,
    reduce_bias,
):
    row_count, sequence, model_width = hidden.shape
    head_count = HEADS
    head_width = model_width // head_count
    score_scale = head_width ** (-0.5)
    query_count = GROUPS * QUERIES
    inner_width = reduce_weight.shape[0] // 2
    token_count = row_count * sequence
    flat_hidden = hidden.reshape(token_count, model_width)
    residual = flat_hidden.astype(jnp.float32)
    qkv_bias = jnp.concatenate([self_bias[0], jnp.zeros_like(self_bias[0]), self_bias[1]])
    qkv_low = (
        (product(flat_hidden, self_weight) + qkv_bias)
        .astype(jnp.bfloat16)
        .reshape(row_count, sequence, 3, head_count, head_width)
    )
    self_queries = qkv_low[:, :, 0]
    self_keys = qkv_low[:, :, 1]
    self_values = qkv_low[:, :, 2]
    segment = segments(lengths)
    visible = (segment[:, :, None] == segment[:, None, :])[:, None]

    def self_scores():
        raw_scores = jnp.einsum(
            "rqhd,rkhd->rhqk", self_queries, self_keys, preferred_element_type=jnp.float32
        )
        return jnp.where(visible, raw_scores * score_scale, masked_score)

    scores = self_scores()
    row_max = jnp.max(scores, axis=-1, keepdims=True)
    unnormed = jnp.exp(scores - row_max)
    row_total = jnp.sum(unnormed, axis=-1, keepdims=True)
    self_lse = row_max + jnp.log(row_total)
    attended = jnp.einsum(
        "rhqk,rkhd->rqhd",
        (unnormed / row_total).astype(jnp.bfloat16),
        self_values,
        preferred_element_type=jnp.float32,
    )
    attended_low = attended.reshape(token_count, model_width).astype(jnp.bfloat16)
    first_out, normed_one, inverse_one = norm_forward(
        residual + product(attended_low, output_weight) + self_bias[2], norm_gain[0], norm_shift[0]
    )
    first_rows = first_out.reshape(row_count, sequence, model_width)
    first_low = first_out.astype(jnp.bfloat16).reshape(row_count, sequence, model_width)
    query_in = first_low[:, :query_count].reshape(-1, model_width)
    text_in = first_low[:, query_count:].reshape(-1, model_width)
    cross_query = (
        (product(query_in, query_weight) + cross_bias[0])
        .astype(jnp.bfloat16)
        .reshape(row_count, GROUPS, QUERIES, model_width)
    )
    select = (image_order[:, :, None] == jnp.arange(GROUPS, dtype=jnp.int32)[None, None, :]).astype(
        jnp.bfloat16
    )
    by_image = jnp.einsum(
        "rgm,rgqd->rmqd", select, cross_query, preferred_element_type=jnp.float32
    ).astype(jnp.bfloat16)
    kv_bias = jnp.concatenate([jnp.zeros_like(cross_bias[1]), cross_bias[1]])
    projected = product(features.reshape(-1, features.shape[-1]), image_weight) + kv_bias
    image_kv = projected.astype(jnp.bfloat16).reshape(
        features.shape[:3] + (2, head_count, head_width)
    )
    local_count = features.shape[2]
    patch_valid = (
        lax.axis_index("patch") * local_count + jnp.arange(local_count, dtype=jnp.int32)
        < PATCHES - PAD
    )
    cross_in = lax.all_gather(by_image, "patch", axis=0, tiled=True)
    image_scores = cross_scores(cross_in, image_kv[:, :, :, 0], patch_valid, score_scale)
    local_max = jnp.max(image_scores, axis=-1)
    local_total = jnp.sum(jnp.exp(image_scores - local_max[..., None]), axis=-1)
    image_max = lax.pmax(local_max.astype(jnp.bfloat16), "patch").astype(local_max.dtype)
    image_total = lax.psum(
        (local_total * jnp.exp(local_max - image_max)).astype(jnp.bfloat16), "patch"
    ).astype(jnp.float32)
    cross_lse = (image_max + jnp.log(image_total))[..., None]
    partial_out = jnp.einsum(
        "nmhqp,nmphd->nmqhd",
        jnp.exp(image_scores - cross_lse).astype(jnp.bfloat16),
        image_kv[:, :, :, 1],
        preferred_element_type=jnp.float32,
    ).reshape(cross_in.shape)
    cross_out = lax.psum_scatter(
        partial_out.astype(jnp.bfloat16), "patch", scatter_dimension=0, tiled=True
    )
    by_group = (
        jnp.einsum("rgm,rmqd->rgqd", select, cross_out, preferred_element_type=jnp.float32)
        .astype(jnp.bfloat16)
        .reshape(-1, model_width)
    )
    query_first = first_rows[:, :query_count].reshape(-1, model_width)
    second_out, normed_two, inverse_two = norm_forward(
        query_first + product(by_group, cross_weight) + cross_bias[2], norm_gain[1], norm_shift[1]
    )
    second_low = second_out.astype(jnp.bfloat16)

    def feed_forward(inputs, residual_in, branch):
        offset = branch * inner_width
        preact = (
            product(inputs, expand_weight[:, offset : offset + inner_width])
            + expand_bias[offset : offset + inner_width]
        )
        active = jax.nn.gelu(preact, approximate=False).astype(jnp.bfloat16)
        summed = (
            residual_in
            + product(active, reduce_weight[offset : offset + inner_width])
            + reduce_bias[branch]
        )
        output, normed, inverse = norm_forward(
            summed, norm_gain[2 + branch], norm_shift[2 + branch]
        )
        return (output, (preact, active, normed, inverse))

    query_final, query_kept = feed_forward(second_low, second_out, 0)
    text_first = first_rows[:, query_count:].reshape(-1, model_width)
    text_final, text_kept = feed_forward(text_in, text_first, 1)
    mixed = jnp.concatenate(
        [
            query_final.reshape(row_count, query_count, model_width),
            text_final.reshape(row_count, -1, model_width),
        ],
        axis=1,
    ).astype(jnp.bfloat16)
    slopes = cotangent.astype(jnp.float32)

    def feed_backward(slope_in, inputs, kept, branch):
        preact, active, normed, inverse = kept
        offset = branch * inner_width
        summed_slope, gain_slope, shift_slope = norm_backward(
            slope_in, normed, inverse, norm_gain[2 + branch]
        )
        summed_low = summed_slope.astype(jnp.bfloat16)
        reduce_slope = weight_gradient(active, summed_low)
        pre_slope = input_gradient(
            summed_low, reduce_weight[offset : offset + inner_width]
        ) * gelu_slope(preact)
        pre_low = pre_slope.astype(jnp.bfloat16)
        expand_slope = weight_gradient(inputs, pre_low)
        inputs_slope = summed_slope + input_gradient(
            pre_low, expand_weight[:, offset : offset + inner_width]
        )
        return (
            inputs_slope,
            expand_slope,
            reduce_slope,
            jnp.sum(pre_slope, axis=0),
            jnp.sum(summed_slope, axis=0),
            gain_slope,
            shift_slope,
        )

    query_back = feed_backward(
        slopes[:, :query_count].reshape(-1, model_width), second_low, query_kept, 0
    )
    text_back = feed_backward(
        slopes[:, query_count:].reshape(-1, model_width), text_in, text_kept, 1
    )
    second_slope, gain_two, shift_two = norm_backward(
        query_back[0], normed_two, inverse_two, norm_gain[1]
    )
    second_low_slope = second_slope.astype(jnp.bfloat16)
    cross_weight_slope = weight_gradient(by_group, second_low_slope)
    group_slope = (
        input_gradient(second_low_slope, cross_weight)
        .astype(jnp.bfloat16)
        .reshape(row_count, GROUPS, QUERIES, model_width)
    )
    image_slope = jnp.einsum(
        "rgm,rgqd->rmqd", select, group_slope, preferred_element_type=jnp.float32
    ).astype(jnp.bfloat16)
    slope_all = lax.all_gather(image_slope, "patch", axis=0, tiled=True)
    image_probs = jnp.exp(
        cross_scores(cross_in, image_kv[:, :, :, 0], patch_valid, score_scale) - cross_lse
    )
    prob_slopes = jnp.einsum(
        "nmqhd,nmphd->nmhqp",
        split_heads(slope_all, head_count),
        image_kv[:, :, :, 1],
        preferred_element_type=jnp.float32,
    )
    image_delta = lax.psum(
        jnp.sum(image_probs * prob_slopes, axis=-1).astype(jnp.bfloat16), "patch"
    ).astype(jnp.float32)[..., None]
    partial_slope, kv_slope, value_bias_slope = score_slopes(
        image_probs, prob_slopes, image_delta, cross_in, image_kv, slope_all, score_scale
    )
    query_slope = lax.psum_scatter(
        partial_slope.astype(jnp.bfloat16), "patch", scatter_dimension=0, tiled=True
    ).astype(jnp.float32)
    image_weight_slope = weight_gradient(features.reshape(-1, features.shape[-1]), kv_slope)
    query_bias_slope = jnp.sum(query_slope, axis=(0, 1, 2))
    query_low = query_slope.astype(jnp.bfloat16)
    group_query = (
        jnp.einsum("rgm,rmqd->rgqd", select, query_low, preferred_element_type=jnp.float32)
        .astype(jnp.bfloat16)
        .reshape(-1, model_width)
    )
    query_weight_slope = weight_gradient(query_in, group_query)
    query_rows_slope = second_slope + input_gradient(group_query, query_weight)
    first_slope = jnp.concatenate(
        [
            query_rows_slope.reshape(row_count, query_count, model_width),
            text_back[0].reshape(row_count, -1, model_width),
        ],
        axis=1,
    ).reshape(token_count, model_width)
    one_slope, gain_one, shift_one = norm_backward(
        first_slope, normed_one, inverse_one, norm_gain[0]
    )
    one_low = one_slope.astype(jnp.bfloat16)
    output_weight_slope = weight_gradient(attended_low, one_low)
    attend_slope = (
        input_gradient(one_low, output_weight)
        .astype(jnp.bfloat16)
        .reshape(row_count, sequence, head_count, head_width)
    )
    self_probs = jnp.exp(self_scores() - self_lse)
    self_prob_slopes = jnp.einsum(
        "rqhd,rkhd->rhqk", attend_slope, self_values, preferred_element_type=jnp.float32
    )
    self_delta = jnp.sum(self_probs * self_prob_slopes, axis=-1, keepdims=True)
    self_score_low = (self_probs * (self_prob_slopes - self_delta) * score_scale).astype(
        jnp.bfloat16
    )
    self_query_slope = jnp.einsum(
        "rhqk,rkhd->rqhd", self_score_low, self_keys, preferred_element_type=jnp.float32
    )
    self_key_slope = jnp.einsum(
        "rhqk,rqhd->rkhd", self_score_low, self_queries, preferred_element_type=jnp.float32
    )
    self_value_slope = jnp.einsum(
        "rhqk,rqhd->rkhd",
        self_probs.astype(jnp.bfloat16),
        attend_slope,
        preferred_element_type=jnp.float32,
    )
    qkv_slope = jnp.stack([self_query_slope, self_key_slope, self_value_slope], axis=2).reshape(
        token_count, 3 * model_width
    )
    qkv_sums = jnp.sum(qkv_slope, axis=0)
    qkv_low_slope = qkv_slope.astype(jnp.bfloat16)
    self_weight_slope = weight_gradient(flat_hidden, qkv_low_slope)
    hidden_gradient = (
        (one_slope + input_gradient(qkv_low_slope, self_weight))
        .astype(jnp.bfloat16)
        .reshape(row_count, sequence, model_width)
    )
    expand_slope = jnp.concatenate([query_back[1], text_back[1]], axis=1)
    reduce_slope = jnp.concatenate([query_back[2], text_back[2]], axis=0)
    row_sums = (
        lax.psum_scatter(
            self_weight_slope.astype(jnp.bfloat16), "dp", scatter_dimension=0, tiled=True
        ).astype(jnp.float32),
        lax.psum_scatter(
            output_weight_slope.astype(jnp.bfloat16), "dp", scatter_dimension=0, tiled=True
        ).astype(jnp.float32),
        lax.psum_scatter(
            query_weight_slope.astype(jnp.bfloat16), "dp", scatter_dimension=0, tiled=True
        ).astype(jnp.float32),
        lax.psum_scatter(
            image_weight_slope.astype(jnp.bfloat16), "dp", scatter_dimension=0, tiled=True
        ).astype(jnp.float32),
        lax.psum_scatter(
            cross_weight_slope.astype(jnp.bfloat16), "dp", scatter_dimension=0, tiled=True
        ).astype(jnp.float32),
        lax.psum_scatter(
            expand_slope.astype(jnp.bfloat16), "dp", scatter_dimension=0, tiled=True
        ).astype(jnp.float32),
        lax.psum_scatter(
            reduce_slope.astype(jnp.bfloat16), "dp", scatter_dimension=0, tiled=True
        ).astype(jnp.float32),
    )
    self_part, output_part, query_part, image_part, cross_part, expand_part, reduce_part = row_sums
    summed = (
        lax.psum_scatter(
            self_part.astype(jnp.bfloat16), "patch", scatter_dimension=1, tiled=True
        ).astype(jnp.float32),
        lax.psum_scatter(
            output_part.astype(jnp.bfloat16), "patch", scatter_dimension=1, tiled=True
        ).astype(jnp.float32),
        lax.psum_scatter(
            query_part.astype(jnp.bfloat16), "patch", scatter_dimension=1, tiled=True
        ).astype(jnp.float32),
        lax.psum_scatter(
            image_part.astype(jnp.bfloat16), "patch", scatter_dimension=1, tiled=True
        ).astype(jnp.float32),
        lax.psum_scatter(
            cross_part.astype(jnp.bfloat16), "patch", scatter_dimension=1, tiled=True
        ).astype(jnp.float32),
        lax.psum_scatter(
            expand_part.astype(jnp.bfloat16), "patch", scatter_dimension=1, tiled=True
        ).astype(jnp.float32),
        lax.psum_scatter(
            reduce_part.astype(jnp.bfloat16), "patch", scatter_dimension=1, tiled=True
        ).astype(jnp.float32),
    )
    vectors = lax.psum(
        (
            jnp.stack(
                [qkv_sums[:model_width], qkv_sums[2 * model_width :], jnp.sum(one_slope, axis=0)]
            ),
            jnp.stack([gain_one, gain_two, query_back[5], text_back[5]]),
            jnp.stack([shift_one, shift_two, query_back[6], text_back[6]]),
            jnp.stack([query_bias_slope, value_bias_slope, jnp.sum(second_slope, axis=0)]),
            jnp.concatenate([query_back[3], text_back[3]]),
            jnp.stack([query_back[4], text_back[4]]),
        ),
        ("dp", "patch"),
    )
    return (
        mixed,
        hidden_gradient,
        summed[0],
        summed[1],
        vectors[0],
        vectors[1],
        vectors[2],
        summed[2],
        summed[3],
        summed[4],
        vectors[3],
        summed[5],
        vectors[4],
        summed[6],
        vectors[5],
    )


def solution(mesh):
    placed = (
        P(("dp", "patch"), None, None),
        P(("dp", "patch"), None),
        P(("dp", "patch"), None),
        P("dp", None, "patch", None),
        P(("dp", "patch"), None, None),
        P(),
        P(),
        P(),
        P(),
        P(),
        P(),
        P(),
        P(),
        P(),
        P(),
        P(),
        P(),
        P(),
    )
    return jax.shard_map(
        local,
        mesh=mesh,
        in_specs=placed,
        out_specs=(
            P(("dp", "patch"), None, None),
            P(("dp", "patch"), None, None),
            P("dp", "patch"),
            P("dp", "patch"),
            P(),
            P(),
            P(),
            P("dp", "patch"),
            P("dp", "patch"),
            P("dp", "patch"),
            P(),
            P("dp", "patch"),
            P(),
            P("dp", "patch"),
            P(),
        ),
        check_vma=False,
    )
```

profile of v0, /device:TPU:8, one launch (start us, length us, event | category | flops | bytes accessed | tf_op | source)
XLA Modules:
  0.0 1143.9 jit_solution(15614863307356175441)
XLA Ops:
  58.8 15.7 %fusion.1 = bf16[2112,1536]{1,0:T(8,128)(2,1)} fusion(bf16[2112,1408]{1,0:T(8,128)(2,1)} %reshape.304, bf16[1408,1536]{1,0:T(8,128)(2,1)} %param.29, f32[1536]{0:T(1024)S(1)} %concatenate.29), kind=kOutput, calls=%fused_computation.5 | convolution fusion | flops 9141682176 | bytes 16766976 | tf_op jit(solution)/shard_map/dot_general | solution.py:19
  74.6 21.7 %reshape.340 = bf16[4,4,132,2,12,64]{5,4,3,2,1,0:T(8,128)(2,1)} reshape(bf16[2112,1536]{1,0:T(8,128)(2,1)} %fusion.1) | data formatting | bytes 12976128 | tf_op jit(solution)/shard_map/reshape | solution.py:192
  96.2 12.4 %fusion.197 = (bf16[4,4,132,1,12,64]{5,4,3,2,1,0:T(8,128)(2,1)}, bf16[4,4,132,1,12,64]{5,4,3,2,1,0:T(8,128)(2,1)}) fusion(bf16[4,4,132,2,12,64]{5,4,3,2,1,0:T(8,128)(2,1)} %reshape.340), kind=kLoop, calls=%fused_computation.296 | loop fusion | bytes 12976128 | tf_op jit(solution)/shard_map/slice | solution.py:201
  108.7 14.1 %copy.190 = bf16[4,4,132,1,12,64]{2,5,4,1,0,3:T(8,128)(2,1)} copy(bf16[4,4,132,1,12,64]{5,4,3,2,1,0:T(8,128)(2,1)} %get-tuple-element.122) | data formatting | bytes 6488064
  123.3 14.1 %copy.191 = bf16[4,4,132,1,12,64]{2,5,4,1,0,3:T(8,128)(2,1)} copy(bf16[4,4,132,1,12,64]{5,4,3,2,1,0:T(8,128)(2,1)} %get-tuple-element.121) | data formatting | bytes 6488064
  142.6 11.6 %all_gather.6 = bf16[4,4,32,768]{3,2,1,0:T(8,128)(2,1)} all-gather(bf16[2,4,32,768]{3,2,1,0:T(8,128)(2,1)S(1)} %copy.137), channel_id=1, replica_groups=mesh['dp'=16,'patch'=2] {'patch'}, dimensions={0}, use_global_device_ids=true | all-gather | bytes 1179648 | tf_op jit(solution)/shard_map/all_gather | solution.py:200
  209.6 10.7 fusion.62
  270.1 10.6 multiply_reduce_fusion.1
  280.7 10.4 psum.57
  368.8 21.2 %convert_element_type.270 = bf16[2112,1536]{0,1:T(8,128)(2,1)} reshape(bf16[4,4,132,2,12,64]{2,1,0,5,4,3:T(4,128)(2,1)} %copy.159) | data formatting | bytes 12976128 | tf_op jit(solution)/shard_map/convert_element_type | solution.py:105
  392.9 15.8 %fusion.2 = bf16[1408,1536]{0,1:T(8,128)(2,1)} fusion(bf16[2112,1536]{0,1:T(8,128)(2,1)} %convert_element_type.270, bf16[2112,1408]{1,0:T(8,128)(2,1)} %reshape.304), kind=kOutput, calls=%fused_computation.9 | convolution fusion | flops 9137356800 | bytes 16760832 | tf_op jit(solution)/shard_map/dot_general | solution.py:23
  430.6 13.7 %fusion.103 = f32[2,256,1,12,64]{1,4,3,0,2:T(8,128)} fusion(f32[2,12,256,256]{2,3,1,0:T(8,128)} %fusion.146, f32[2,12,256]{2,1,0:T(8,128)} %log_add_fusion, f32[2,12,256,256]{2,3,1,0:T(8,128)} %copy-done.15, pred[2,256,256]{1,2,0:T(8,128)(4,1)} %broadcast_compare_fusion, bf16[2,256,1,12,64]{1,0,4,3,2:T(2,128)(2,1)} %copy-done.43), kind=kOutput, calls=%fused_computation.140 | convolution fusion | flops 218634496 | bytes 15097856 | tf_op jit(solution)/shard_map/rhqk,rqhd->rkhd/dot_general | solution.py:360
  444.4 13.7 %fusion.100 = f32[2,256,1,12,64]{1,4,3,0,2:T(8,128)} fusion(f32[2,12,256,256]{2,3,1,0:T(8,128)} %fusion.146, f32[2,12,256]{2,1,0:T(8,128)} %log_add_fusion, f32[2,12,256,256]{2,3,1,0:T(8,128)} %copy-done.15, pred[2,256,256]{1,2,0:T(8,128)(4,1)} %broadcast_compare_fusion, bf16[2,256,1,12,64]{1,0,4,3,2:T(2,128)(2,1)} %copy-done.42), kind=kOutput, calls=%fused_computation.139 | convolution fusion | flops 218634496 | bytes 15097856 | tf_op jit(solution)/shard_map/rhqk,rkhd->rqhd/dot_general | solution.py:357
  483.9 15.4 %pad_maximum_fusion.2 = bf16[6144,768]{1,0:T(8,128)(2,1)} fusion(bf16[3072,768]{1,0:T(8,128)(2,1)S(1)} %convolution_convert_fusion.1, bf16[3072,768]{1,0:T(8,128)(2,1)S(1)} %convolution_convert_fusion.2), kind=kLoop, calls=%fused_computation.7 | loop fusion | flops 18874368 | bytes 18874368 | tf_op jit(solution)/shard_map/concatenate | solution.py:381
  513.7 72.1 %reduce-scatter.55.cloned.1.call-done = bf16[88,1536]{1,0:T(8,128)(2,1)} async-done(((bf16[1408,1536]{1,0:T(8,128)(2,1)}), bf16[88,1536]{1,0:T(8,128)(2,1)}) %reduce-scatter.55.cloned.1.call-update) | async-done | bytes 270352
  587.7 69.1 %reduce-scatter.49.cloned.1.call-done = bf16[48,2304]{1,0:T(8,128)(2,1)} async-done(((bf16[768,2304]{1,0:T(8,128)(2,1)}), bf16[48,2304]{1,0:T(8,128)(2,1)}) %reduce-scatter.49.cloned.1.call-update) | async-done | bytes 221200
  658.9 112.9 %reduce-scatter.47.cloned.1.call-done = bf16[384,768]{1,0:T(8,128)(2,1)} async-done(((bf16[6144,768]{1,0:T(8,128)(2,1)}), bf16[384,768]{1,0:T(8,128)(2,1)}) %reduce-scatter.47.cloned.1.call-update) | async-done | bytes 589840 | tf_op jit(solution)/shard_map/reduce_scatter | solution.py:401
  784.9 102.7 %reduce-scatter.43.cloned.1.call-done = bf16[48,6144]{1,0:T(8,128)(2,1)} async-done(((bf16[768,6144]{1,0:T(8,128)(2,1)}), bf16[48,6144]{1,0:T(8,128)(2,1)}) %reduce-scatter.43.cloned.1.call-update) | async-done | bytes 589840 | tf_op jit(solution)/shard_map/reduce_scatter | solution.py:398
  917.1 10.7 reduce-scatter.53.cloned.1.call-done
  930.8 12.4 %reduce-scatter.39.cloned.1.call-done = bf16[88,768]{0,1:T(8,128)(2,1)} async-done(((bf16[88,1536]{0,1:T(8,128)(2,1)}), bf16[88,768]{0,1:T(8,128)(2,1)}) %reduce-scatter.39.cloned.1.call-update) | async-done | bytes 135184 | tf_op jit(solution)/shard_map/reduce_scatter | solution.py:416
  944.9 16.4 %reduce-scatter.33.cloned.1.call-done = bf16[48,1152]{0,1:T(8,128)(2,1)} async-done(((bf16[48,2304]{0,1:T(8,128)(2,1)}), bf16[48,1152]{0,1:T(8,128)(2,1)}) %reduce-scatter.33.cloned.1.call-update) | async-done | bytes 110608 | tf_op jit(solution)/shard_map/reduce_scatter | solution.py:407
  963.1 16.2 %reduce-scatter.59.cloned.1.call-done = bf16[384,384]{1,0:T(8,128)(2,1)} async-done(((bf16[768,384]{1,0:T(8,128)(2,1)}), bf16[384,384]{1,0:T(8,128)(2,1)}) %reduce-scatter.59.cloned.1.call-update) | async-done | bytes 294928
  982.9 13.8 %reduce-scatter.45.cloned.1.call-done = bf16[48,3072]{1,0:T(8,128)(2,1)} async-done(((bf16[48,6144]{1,0:T(8,128)(2,1)}), bf16[48,3072]{1,0:T(8,128)(2,1)}) %reduce-scatter.45.cloned.1.call-update) | async-done | bytes 294928 | tf_op jit(solution)/shard_map/reduce_scatter | solution.py:422
  998.6 130.8 %all-reduce.4.cloned.1.call-done = (f32[3,768]{1,0:T(4,128)}, f32[4,768]{1,0:T(4,128)}, f32[4,768]{1,0:T(4,128)}, f32[3,768]{1,0:T(4,128)}, f32[6144]{0:T(1024)}, /*index=5*/f32[2,768]{1,0:T(2,128)}) async-done(((f32[3,768]{1,0:T(4,128)}, f32[4,768]{1,0:T(4,128)}, f32[4,768]{1,0:T(4,128)}, f32[3,768]{1,0:T(4,128)}, f32[6144]{0:T(1024)}, /*index=5*/f32[2,768]{1,0:T(2,128)}), (f32[3,768]{1,0:T(4,128)}, ...) | async-done | bytes 73744 | tf_op jit(solution)/shard_map/psum | solution.py:429
  (395 shorter events, 370.2 us)
Async XLA Ops:
  7.2 222.7 %reduce-scatter.29.cloned.1.call-start = ((), (), s32[]{:S(2)}) async-start(), calls=%async_computation.16 | async-start | bytes 1179648 | tf_op jit(solution)/shard_map/reduce_scatter | solution.py:215
  204.5 122.9 %reduce-scatter.31.cloned.1.call-start = ((), (), s32[]{:S(2)}) async-start(), calls=%async_computation.17 | async-start | bytes 1179648 | tf_op jit(solution)/shard_map/reduce_scatter | solution.py:319
  229.9 14.3 %slice-start.2 = ((s8[9437184]{0:T(1024)(128)(4,1)}), s8[4194304]{0:T(1024)(128)(4,1)S(1)}, s32[]{:S(2)}) async-start(s8[9437184]{0:T(1024)(128)(4,1)} %bitcast.236), calls=%async_computation.35 | async-start | bytes 8388608
  233.8 21.1 %copy-start.6 = (f32[256,768]{1,0:T(8,128)}, f32[256,768]{1,0:T(8,128)S(1)}, u32[]{:S(2)}) copy-start(f32[256,768]{1,0:T(8,128)S(1)} %get-tuple-element.151) | copy-start | bytes 2359300
  233.8 21.0 %copy-start.54 = (f32[256]{0:T(256)}, f32[256]{0:T(256)S(1)}, u32[]{:S(2)}) copy-start(f32[256]{0:T(256)S(1)} %broadcast_multiply_fusion.8) | copy-start | bytes 3076
  234.0 20.8 %copy-start.63 = (f32[256]{0:T(256)}, f32[256]{0:T(256)S(1)}, u32[]{:S(2)}) copy-start(f32[256]{0:T(256)S(1)} %add_rsqrt_fusion.3) | copy-start | bytes 3076
  257.1 13.0 %copy-start.56 = (pred[132]{0:T(512)(128)(4,1)S(1)}, pred[132]{0:T(512)(128)(4,1)}, u32[]{:S(2)}) copy-start(pred[132]{0:T(512)(128)(4,1)} %add_compare_fusion) | copy-start | bytes 400
  309.6 198.7 %reduce-scatter.41.cloned.1.call-start = ((), (), s32[]{:S(2)}) async-start(), calls=%async_computation.22 | async-start | bytes 1253376 | tf_op jit(solution)/shard_map/reduce_scatter | solution.py:395
  324.2 185.9 %reduce-scatter.35.cloned.1.call-start = ((), (), s32[]{:S(2)}) async-start(), calls=%async_computation.19 | async-start | bytes 1253376 | tf_op jit(solution)/shard_map/reduce_scatter | solution.py:386
  337.3 174.6 %reduce-scatter.37.cloned.1.call-start = ((), (), s32[]{:S(2)}) async-start(), calls=%async_computation.20 | async-start | bytes 1253376 | tf_op jit(solution)/shard_map/reduce_scatter | solution.py:389
  392.8 192.9 %reduce-scatter.55.cloned.1.call-start = ((), (), s32[]{:S(2)}) async-start(), calls=%async_computation.29 | async-start | bytes 4595712
  415.3 241.5 %reduce-scatter.49.cloned.1.call-start = ((), (), s32[]{:S(2)}) async-start(), calls=%async_computation.26 | async-start | bytes 3760128
  479.0 292.7 %reduce-scatter.47.cloned.1.call-start = ((), (), s32[]{:S(2)}) async-start(), calls=%async_computation.25 | async-start | bytes 10027008 | tf_op jit(solution)/shard_map/reduce_scatter | solution.py:401
  499.3 388.3 %reduce-scatter.43.cloned.1.call-start = ((), (), s32[]{:S(2)}) async-start(), calls=%async_computation.23 | async-start | bytes 10027008 | tf_op jit(solution)/shard_map/reduce_scatter | solution.py:398
  508.2 267.1 %copy-start.58 = (f32[768]{0:T(1024)S(1)}, f32[768]{0:T(1024)}, u32[]{:S(2)}) copy-start(f32[768]{0:T(1024)} %get-tuple-element.86) | copy-start | bytes 9220
  508.2 267.7 %copy-start.57 = (f32[768]{0:T(1024)S(1)}, f32[768]{0:T(1024)}, u32[]{:S(2)}) copy-start(f32[768]{0:T(1024)} %get-tuple-element.83) | copy-start | bytes 9220
  508.2 399.7 %reduce-scatter.57.cloned.1.call-start = ((), (), s32[]{:S(2)}) async-start(), calls=%async_computation.30 | async-start | bytes 294912
  510.0 404.1 %reduce-scatter.51.cloned.1.call-start = ((), (), s32[]{:S(2)}) async-start(), calls=%async_computation.27 | async-start | bytes 294912
  511.8 416.0 %reduce-scatter.53.cloned.1.call-start = ((), (), s32[]{:S(2)}) async-start(), calls=%async_computation.28 | async-start | bytes 294912
  513.6 429.5 %reduce-scatter.39.cloned.1.call-start = ((), (), s32[]{:S(2)}) async-start(), calls=%async_computation.21 | async-start | bytes 589824 | tf_op jit(solution)/shard_map/reduce_scatter | solution.py:416
  587.6 373.6 %reduce-scatter.33.cloned.1.call-start = ((), (), s32[]{:S(2)}) async-start(), calls=%async_computation.18 | async-start | bytes 884736 | tf_op jit(solution)/shard_map/reduce_scatter | solution.py:407
  658.8 320.4 %reduce-scatter.59.cloned.1.call-start = ((), (), s32[]{:S(2)}) async-start(), calls=%async_computation.31 | async-start | bytes 884736
  773.9 222.8 %reduce-scatter.45.cloned.1.call-start = ((), (), s32[]{:S(2)}) async-start(), calls=%async_computation.24 | async-start | bytes 884736 | tf_op jit(solution)/shard_map/reduce_scatter | solution.py:422
  887.6 241.7 %all-reduce.4.cloned.1.call-start = ((), (), s32[]{:S(2)}) async-start(), calls=%async_computation.32 | async-start | bytes 159744 | tf_op jit(solution)/shard_map/psum | solution.py:429
  (81 other events, 290.5 us)
Sparse Core Ops, SparseCore 0:
  204.6 18.5 reduce-scatter.28
  309.7 17.6 reduce-scatter.30
  331.0 57.9 reduce-scatter.40
  392.5 57.1 reduce-scatter.34
  453.1 57.1 reduce-scatter.36
  513.9 71.7 reduce-scatter.54
  589.6 67.1 reduce-scatter.48
  660.9 110.8 reduce-scatter.46
  776.4 111.1 reduce-scatter.42
  889.7 10.5 reduce-scatter.56
  903.1 10.9 reduce-scatter.50
  916.8 10.9 reduce-scatter.52
  930.0 13.1 reduce-scatter.38
  945.9 15.2 reduce-scatter.32
  963.9 15.2 reduce-scatter.58
  981.5 15.2 reduce-scatter.44
  1004.2 125.1 all-reduce.3
where the time goes:
time: 1160 us; the launch traced here: 1140 us
  waiting for transfers between devices  564 us (49%)
  local copies, waits for them, and re-layouts  229 us (20%)
  matrix products  201 us (17%)
  other arithmetic  84 us (7%)
  blocking collectives  49.7 us (4%)
  between operations  15.4 us (1%)
    unnamed x23, waiting for transfers between devices  172 us
    psum x1, waiting for transfers between devices, local(): lax.psum((jnp.stack([qkv_sums[:model_width], qkv_sums[2 * model_width:],...  131 us
    reduce_scatter x1, waiting for transfers between devices, local(): lax.psum_scatter(reduce_slope.astype(jnp.bfloat16), 'dp', scatter_dimensi...  113 us
    reduce_scatter x1, waiting for transfers between devices, local(): lax.psum_scatter(expand_slope.astype(jnp.bfloat16), 'dp', scatter_dimensi...  103 us
    unnamed x202, local copies, waits for them, and re-layouts  84.6 us
    dot_general x9, matrix products, product(): return jnp.dot(left, right, preferred_element_type=jnp.float32)  50.7 us
    dot_general x9, matrix products, weight_gradient(): lax.dot_general(inputs, slopes, (((0,), (0,)), ((), ())), preferred_eleme...  36.3 us
    dot_general x8, matrix products, input_gradient(): lax.dot_general(slopes, weight, (((1,), (1,)), ((), ())), preferred_eleme...  27.5 us
  transfers between devices with their start and end apart: 17, of which 12 were waited for; matrix products, arithmetic and copies ran while one was open for 24% of the time, Pallas kernels for 0%

commit v1 on v0

v1 whole, which is shorter than its diff:
```python
import functools

import jax
import jax.numpy as jnp
from jax import lax
from jax.experimental import pallas as pl
from jax.experimental.pallas import tpu as pltpu
from jax.sharding import PartitionSpec as P

HEADS = 12
QUERIES = 32
GROUPS = 4
TEXT = 128
PATCHES = 264
PAD = 7

epsilon = 1e-06
masked_score = -1000000000.0

F32 = jnp.float32
BF16 = jnp.bfloat16
WIDE = 256
CHUNK = 768
VMEM = 56 * 2**20


def nn(left, right):
    return lax.dot_general(left, right, (((1,), (0,)), ((), ())), preferred_element_type=F32)


def nt(left, right):
    return lax.dot_general(left, right, (((1,), (1,)), ((), ())), preferred_element_type=F32)


def tn(left, right):
    return lax.dot_general(left, right, (((0,), (0,)), ((), ())), preferred_element_type=F32)


def norm(hidden):
    row_mean = jnp.mean(hidden, axis=-1, keepdims=True)
    centered = hidden - row_mean
    inverse = lax.rsqrt(jnp.mean(centered * centered, axis=-1, keepdims=True) + epsilon)
    return centered * inverse, inverse


def norm_backward(slopes, normed, inverse, gain):
    scaled = slopes * gain
    return inverse * (
        scaled
        - jnp.mean(scaled, axis=-1, keepdims=True)
        - normed * jnp.mean(scaled * normed, axis=-1, keepdims=True)
    )


def total(values):
    return jnp.sum(values, axis=0, keepdims=True)


def iota(shape, axis):
    return lax.broadcasted_iota(jnp.int32, shape, axis)


def only_head(values, head):
    lanes = iota(values.shape, 1) >> 6
    return jnp.where(lanes == head, values, jnp.zeros_like(values))


def whole(shape):
    return pl.BlockSpec(shape, lambda *_: (0,) * len(shape))


def params(steps):
    return pltpu.CompilerParams(
        dimension_semantics=("arbitrary",) * steps, vmem_limit_bytes=VMEM
    )


def same_group(lengths, row, sequence):
    first = lengths[row, 0]
    second = first + lengths[row, 1]
    third = second + lengths[row, 2]

    def group(place):
        text = place - GROUPS * QUERIES
        after = (
            (text >= first).astype(jnp.int32)
            + (text >= second).astype(jnp.int32)
            + (text >= third).astype(jnp.int32)
        )
        return jnp.where(text < 0, place >> 5, after)

    keys = group(iota((sequence, 1), 0))
    queries = group(iota((1, sequence), 1))
    return jnp.where(keys == queries, 0.0, masked_score).astype(F32)


def self_forward_kernel(
    lengths, order, x_ref, ws_ref, wo_ref, wq_ref, sb_ref, gain_ref, shift_ref, cb_ref,
    qkv_ref, att_ref, lse_ref, n_ref, inv_ref, low_ref, cq_ref, bias_ref,
):
    row = pl.program_id(0)
    x = x_ref[0]
    sequence, width = x.shape
    bias_ref[...] = same_group(lengths, row, sequence)
    qkv_ref[0, :, :width] = (nn(x, ws_ref[:, :width]) + sb_ref[0:1]).astype(BF16)
    qkv_ref[0, :, width : 2 * width] = nn(x, ws_ref[:, width : 2 * width]).astype(BF16)
    qkv_ref[0, :, 2 * width :] = (nn(x, ws_ref[:, 2 * width :]) + sb_ref[1:2]).astype(BF16)
    scale = (width // HEADS) ** -0.5
    for part in range(width // WIDE):
        at = part * WIDE
        queries = qkv_ref[0, :, at : at + WIDE] * jnp.asarray(scale, BF16)
        keys = qkv_ref[0, :, width + at : width + at + WIDE]
        values = qkv_ref[0, :, 2 * width + at : 2 * width + at + WIDE]
        out = jnp.zeros((sequence, WIDE), F32)
        for head in range(4):
            scores = nt(keys, only_head(queries, head)) + bias_ref[...]
            top = jnp.max(scores, axis=0, keepdims=True)
            weights = jnp.exp(scores - top)
            mass = total(weights)
            lse_ref[0, 4 * part + head : 4 * part + head + 1] = top + jnp.log(mass)
            out += tn((weights * (1.0 / mass)).astype(BF16), only_head(values, head))
        att_ref[0, :, at : at + WIDE] = out.astype(BF16)
    normed, inverse = norm(x.astype(F32) + nn(att_ref[0], wo_ref[...]) + sb_ref[2:3])
    n_ref[0] = normed
    inv_ref[0] = inverse
    low_ref[0] = (normed * gain_ref[0:1] + shift_ref[0:1]).astype(BF16)
    cq = (nn(low_ref[0, : GROUPS * QUERIES], wq_ref[...]) + cb_ref[0:1]).astype(BF16)
    for group in range(GROUPS):
        to = pl.multiple_of(order[row, group] * QUERIES, QUERIES)
        cq_ref[0, pl.ds(to, QUERIES)] = cq[group * QUERIES : (group + 1) * QUERIES]


def self_forward(lengths, order, hidden, ws, wo, wq, sb, gain, shift, cb):
    rows, sequence, width = hidden.shape

    def by_row(*shape):
        return pl.BlockSpec((1, *shape), lambda r, *_: (r,) + (0,) * len(shape))

    def out(dtype, *shape):
        return jax.ShapeDtypeStruct((rows, *shape), dtype)

    queries = GROUPS * QUERIES
    return pl.pallas_call(
        self_forward_kernel,
        grid_spec=pltpu.PrefetchScalarGridSpec(
            num_scalar_prefetch=2,
            grid=(rows,),
            in_specs=[by_row(sequence, width)]
            + [whole(a.shape) for a in (ws, wo, wq, sb, gain, shift, cb)],
            out_specs=[
                by_row(sequence, 3 * width),
                by_row(sequence, width),
                by_row(HEADS, sequence),
                by_row(sequence, width),
                by_row(sequence, 1),
                by_row(sequence, width),
                by_row(queries, width),
            ],
            scratch_shapes=[pltpu.VMEM((sequence, sequence), F32)],
        ),
        out_shape=[
            out(BF16, sequence, 3 * width),
            out(BF16, sequence, width),
            out(F32, HEADS, sequence),
            out(F32, sequence, width),
            out(F32, sequence, 1),
            out(BF16, sequence, width),
            out(BF16, queries, width),
        ],
        compiler_params=params(1),
        cost_estimate=pl.CostEstimate(
            flops=2 * rows * sequence * width * 5 * width, bytes_accessed=10**7, transcendentals=0
        ),
        name="self_forward",
    )(lengths, order, hidden, ws, wo, wq, sb, gain, shift, cb)


def image_kernel(slots, x_ref, w_ref, cb_ref, kv_ref, packed_ref):
    count = x_ref.shape[2]
    width = w_ref.shape[1] // 2

    @pl.when(pl.program_id(0) == 0)
    def _():
        packed_ref[...] = jnp.zeros_like(packed_ref)

    for image in range(GROUPS):
        packed_ref[image * slots : image * slots + count] = x_ref[0, image]
    kv_ref[0, :, :width] = nn(packed_ref[...], w_ref[:, :width]).astype(BF16)
    kv_ref[0, :, width:] = (nn(packed_ref[...], w_ref[:, width:]) + cb_ref[1:2]).astype(BF16)


def image_forward(features, weight, cb, slots):
    rows, images, count, depth = features.shape
    width = weight.shape[1]
    return pl.pallas_call(
        functools.partial(image_kernel, slots),
        grid=(rows,),
        in_specs=[
            pl.BlockSpec((1, images, count, depth), lambda r: (r, 0, 0, 0)),
            whole(weight.shape),
            whole(cb.shape),
        ],
        out_specs=pl.BlockSpec((1, images * slots, width), lambda r: (r, 0, 0)),
        out_shape=jax.ShapeDtypeStruct((rows, images * slots, width), BF16),
        scratch_shapes=[pltpu.VMEM((images * slots, depth), BF16)],
        compiler_params=params(1),
        cost_estimate=pl.CostEstimate(
            flops=2 * rows * images * slots * depth * width, bytes_accessed=10**7, transcendentals=0
        ),
        name="image_forward",
    )(features, weight, cb)


def unused_slots(place, slots, local_count):
    patch = place[1] * local_count + iota((slots, 1), 0)
    used = (iota((slots, 1), 0) < local_count) & (patch < PATCHES - PAD)
    return jnp.where(used, 0.0, masked_score).astype(F32)


def spread_heads(values):
    return jnp.concatenate([only_head(values, head) for head in range(4)], axis=0)


def gather_heads(values):
    rows = values.shape[0] // 4
    result = only_head(values[:rows], 0)
    for head in range(1, 4):
        result += only_head(values[head * rows : (head + 1) * rows], head)
    return result


def cross_forward_kernel(slots, local_count, place, kv_ref, q_ref, o_ref, st_ref):
    width = q_ref.shape[2]
    scale = (width // HEADS) ** -0.5
    unused = unused_slots(place, slots, local_count)
    for image in range(GROUPS):
        rows = slice(image * slots, (image + 1) * slots)
        here = slice(image * QUERIES, (image + 1) * QUERIES)
        scores = []
        for part in range(width // WIDE):
            lanes = slice(part * WIDE, (part + 1) * WIDE)
            queries = q_ref[0, here, lanes] * jnp.asarray(scale, BF16)
            scores.append(nt(kv_ref[0, rows, lanes], spread_heads(queries)))
        scores = jnp.concatenate(scores, axis=1) + unused
        top = jnp.max(scores, axis=0, keepdims=True)
        weights = jnp.exp(scores - top)
        mass = total(weights)
        st_ref[0, image : image + 1] = top
        st_ref[0, GROUPS + image : GROUPS + image + 1] = mass
        probs = (weights * (1.0 / mass)).astype(BF16)
        for part in range(width // WIDE):
            lanes = slice(part * WIDE, (part + 1) * WIDE)
            values = kv_ref[0, rows, width + part * WIDE : width + (part + 1) * WIDE]
            block = slice(part * 4 * QUERIES, (part + 1) * 4 * QUERIES)
            o_ref[0, here, lanes] = gather_heads(tn(probs[:, block], values)).astype(BF16)


def cross_forward(place, kv, queries, slots, local_count):
    rows, length, width = queries.shape
    lanes = HEADS * QUERIES
    return pl.pallas_call(
        functools.partial(cross_forward_kernel, slots, local_count),
        grid_spec=pltpu.PrefetchScalarGridSpec(
            num_scalar_prefetch=1,
            grid=(rows,),
            in_specs=[
                pl.BlockSpec((1, *kv.shape[1:]), lambda r, place: (place[0] + r, 0, 0)),
                pl.BlockSpec((1, length, width), lambda r, _: (r, 0, 0)),
            ],
            out_specs=[
                pl.BlockSpec((1, length, width), lambda r, _: (r, 0, 0)),
                pl.BlockSpec((1, 2 * GROUPS, lanes), lambda r, _: (r, 0, 0)),
            ],
        ),
        out_shape=[
            jax.ShapeDtypeStruct((rows, length, width), BF16),
            jax.ShapeDtypeStruct((rows, 2 * GROUPS, lanes), F32),
        ],
        compiler_params=params(1),
        cost_estimate=pl.CostEstimate(
            flops=rows * 2 * 10**9, bytes_accessed=rows * 2 * 10**6, transcendentals=0
        ),
        name="cross_forward",
    )(place, kv, queries)


def cross_backward_kernel(
    slots, local_count, place, kv_ref, q_ref, do_ref, ld_ref, dq_ref, dkv_ref, sum_ref
):
    width = q_ref.shape[2]
    scale = (width // HEADS) ** -0.5
    unused = unused_slots(place, slots, local_count)

    @pl.when(pl.program_id(0) == 0)
    def _():
        sum_ref[...] = jnp.zeros_like(sum_ref)

    for image in range(GROUPS):
        rows = slice(image * slots, (image + 1) * slots)
        here = slice(image * QUERIES, (image + 1) * QUERIES)
        lse = ld_ref[0, image : image + 1]
        delta = ld_ref[0, GROUPS + image : GROUPS + image + 1]
        for part in range(width // WIDE):
            lanes = slice(part * WIDE, (part + 1) * WIDE)
            vlanes = slice(width + part * WIDE, width + (part + 1) * WIDE)
            block = slice(part * 4 * QUERIES, (part + 1) * 4 * QUERIES)
            queries = spread_heads(q_ref[0, here, lanes])
            slopes = spread_heads(do_ref[0, here, lanes])
            keys = kv_ref[0, rows, lanes]
            values = kv_ref[0, rows, vlanes]
            scores = nt(keys, queries * jnp.asarray(scale, BF16)) + unused
            probs = jnp.exp(scores - lse[:, block])
            prob_slopes = nt(values, slopes)
            low = (probs * (prob_slopes - delta[:, block]) * scale).astype(BF16)
            value_slope = nn(probs.astype(BF16), slopes)
            sum_ref[:, lanes] += total(value_slope)
            dkv_ref[0, rows, lanes] = nn(low, queries).astype(BF16)
            dkv_ref[0, rows, vlanes] = value_slope.astype(BF16)
            dq_ref[0, here, lanes] = gather_heads(tn(low, keys)).astype(BF16)


def cross_backward(place, kv, queries, slopes, ld, slots, local_count):
    rows, length, width = queries.shape
    lanes = HEADS * QUERIES
    by_row = pl.BlockSpec((1, length, width), lambda r, _: (r, 0, 0))
    return pl.pallas_call(
        functools.partial(cross_backward_kernel, slots, local_count),
        grid_spec=pltpu.PrefetchScalarGridSpec(
            num_scalar_prefetch=1,
            grid=(rows,),
            in_specs=[
                pl.BlockSpec((1, *kv.shape[1:]), lambda r, place: (place[0] + r, 0, 0)),
                by_row,
                by_row,
                pl.BlockSpec((1, 2 * GROUPS, lanes), lambda r, _: (r, 0, 0)),
            ],
            out_specs=[
                by_row,
                pl.BlockSpec((1, *kv.shape[1:]), lambda r, _: (r, 0, 0)),
                pl.BlockSpec((1, width), lambda r, _: (0, 0)),
            ],
        ),
        out_shape=[
            jax.ShapeDtypeStruct((rows, length, width), BF16),
            jax.ShapeDtypeStruct((rows, *kv.shape[1:]), BF16),
            jax.ShapeDtypeStruct((1, width), F32),
        ],
        compiler_params=params(1),
        cost_estimate=pl.CostEstimate(
            flops=rows * 4 * 10**9, bytes_accessed=rows * 4 * 10**6, transcendentals=0
        ),
        name="cross_backward",
    )(place, kv, queries, slopes, ld)


def feed_forward_step(ffn, step, z, we, be, wr):
    act_ref, slope_ref, sum_ref = ffn
    pre = nn(z, we) + be
    phi = 0.5 * (1.0 + lax.erf(pre * 0.7071067811865476))
    act = (pre * phi).astype(BF16)
    act_ref[:, pl.ds(pl.multiple_of(step * CHUNK, 128), CHUNK)] = act
    slope_ref[step] = phi + pre * jnp.exp(-0.5 * pre * pre) * 0.3989422804014327
    part = nn(act, wr)

    @pl.when(step == 0)
    def _():
        sum_ref[...] = part

    @pl.when(step > 0)
    def _():
        sum_ref[...] += part


def feed_backward_step(stack_ref, be_slope_ref, slope_ref, sum_ref, step, first, dh_low, we, wr, at):
    pre_slope = nt(dh_low, wr) * slope_ref[step]
    lanes = pl.multiple_of(step * CHUNK, 128)
    be_slope_ref[:, pl.ds(lanes, CHUNK)] = total(pre_slope)
    low = pre_slope.astype(BF16)
    stack_ref[:, pl.ds(at + lanes, CHUNK)] = low
    part = nt(low, we)

    @pl.when(first)
    def _():
        sum_ref[...] = part

    @pl.when(jnp.logical_not(first))
    def _():
        sum_ref[...] += part


def text_kernel(
    n_ref, low_ref, cot_ref, we_ref, be_ref, wr_ref, br_ref, gain_ref, shift_ref,
    mixed_ref, stack_ref, dz_ref, be_slope_ref, vec_ref, slope_ref, sum_ref, dh_ref,
):
    phase, step = pl.program_id(0), pl.program_id(1)
    steps = pl.num_programs(1)
    rows, length, width = n_ref.shape
    inner = be_slope_ref.shape[1]
    tokens = rows * length
    z = low_ref[...].reshape(tokens, width)

    @pl.when(phase == 0)
    def _():
        feed_forward_step(
            (stack_ref, slope_ref, sum_ref), step, z, we_ref[...], be_ref[...], wr_ref[...]
        )

    @pl.when((phase == 1) & (step == 0))
    def _():
        stack_ref[:, 2 * inner : 2 * inner + width] = z
        residual = n_ref[...].reshape(tokens, width) * gain_ref[0:1] + shift_ref[0:1]
        normed, inverse = norm(residual + sum_ref[...] + br_ref[1:2])
        mixed = normed * gain_ref[3:4] + shift_ref[3:4]
        mixed_ref[...] = mixed.astype(BF16).reshape(rows, length, width)
        slopes = cot_ref[...].reshape(tokens, width).astype(F32)
        dh = norm_backward(slopes, normed, inverse, gain_ref[3:4])
        vec_ref[...] = jnp.zeros_like(vec_ref)
        vec_ref[0:1] = total(dh)
        vec_ref[1:2] = total(slopes * normed)
        vec_ref[2:3] = total(slopes)
        dh_ref[...] = dh
        stack_ref[:, 2 * inner + width : 2 * inner + 2 * width] = dh.astype(BF16)

    @pl.when(phase == 1)
    def _():
        feed_backward_step(
            stack_ref, be_slope_ref, slope_ref, sum_ref, steps - 1 - step, step == 0,
            stack_ref[:, 2 * inner + width : 2 * inner + 2 * width], we_ref[...], wr_ref[...], inner,
        )

    @pl.when((phase == 1) & (step == steps - 1))
    def _():
        dz_ref[...] = (dh_ref[...] + sum_ref[...]).reshape(rows, length, width)


def branch_specs(branch, steps, width):
    def turn(phase, step):
        return branch * steps + jnp.where(phase == 0, step, steps - 1 - step)

    return [
        pl.BlockSpec((width, CHUNK), lambda p, s, *_: (0, turn(p, s))),
        pl.BlockSpec((1, CHUNK), lambda p, s, *_: (0, turn(p, s))),
        pl.BlockSpec((CHUNK, width), lambda p, s, *_: (turn(p, s), 0)),
    ]


def text_branch(n1, low1, cot, we, be, wr, br, gain, shift):
    rows, sequence, width = n1.shape
    inner = we.shape[1] // 2
    steps = inner // CHUNK
    tokens = rows * TEXT
    half = pl.BlockSpec((rows, TEXT, width), lambda *_: (0, 1, 0))
    wide = 2 * inner + 2 * width
    return pl.pallas_call(
        text_kernel,
        grid=(2, steps),
        in_specs=[half, half, half]
        + branch_specs(1, steps, width)
        + [whole(br.shape), whole(gain.shape), whole(shift.shape)],
        out_specs=[
            half,
            whole((tokens, wide)),
            whole((rows, TEXT, width)),
            whole((1, inner)),
            whole((8, width)),
        ],
        out_shape=[
            jax.ShapeDtypeStruct((rows, sequence, width), BF16),
            jax.ShapeDtypeStruct((tokens, wide), BF16),
            jax.ShapeDtypeStruct((rows, TEXT, width), F32),
            jax.ShapeDtypeStruct((1, inner), F32),
            jax.ShapeDtypeStruct((8, width), F32),
        ],
        scratch_shapes=[
            pltpu.VMEM((steps, tokens, CHUNK), F32),
            pltpu.VMEM((tokens, width), F32),
            pltpu.VMEM((tokens, width), F32),
        ],
        compiler_params=params(2),
        cost_estimate=pl.CostEstimate(
            flops=16 * tokens * width * inner, bytes_accessed=2 * 10**7, transcendentals=0
        ),
        name="text_branch",
    )(n1, low1, cot, we, be, wr, br, gain, shift)


def head_map(width):
    shape = (HEADS * QUERIES, width)
    return (iota(shape, 0) // QUERIES == iota(shape, 1) // (width // HEADS)).astype(BF16)


def own_query(tokens):
    shape = (tokens, HEADS * QUERIES)
    return (iota(shape, 0) & (QUERIES - 1)) == (iota(shape, 1) & (QUERIES - 1))


def two_terms(values):
    high = values.astype(BF16)
    return high, (values - high.astype(F32)).astype(BF16)


def query_kernel(
    order, o_ref, po_ref, st_ref, pst_ref, n_ref, cot_ref, we_ref, be_ref, wr_ref, br_ref,
    gain_ref, shift_ref, wx_ref, cb_ref, _,
    mixed_ref, stack_ref, dh2_ref, dca_ref, ld_ref, be_slope_ref, vec_ref,
    slope_ref, sum_ref, dh_ref, out_ref, x2_ref, n2_ref, inv2_ref, map_ref,
):
    phase, step = pl.program_id(0), pl.program_id(1)
    steps = pl.num_programs(1)
    rows, length, width = n_ref.shape
    inner = be_slope_ref.shape[1]
    tokens = rows * length
    zs = slice(2 * inner, 2 * inner + width)
    dhs = slice(2 * inner + width, 2 * inner + 2 * width)
    cas = slice(2 * inner + 2 * width, 2 * inner + 3 * width)
    dh2s = slice(2 * inner + 3 * width, 2 * inner + 4 * width)

    @pl.when((phase == 0) & (step == 0))
    def _():
        map_ref[...] = head_map(width)
        shares, other_shares = [], []
        for row in range(rows):
            top, other_top = st_ref[row, :GROUPS], pst_ref[row, :GROUPS]
            both = jnp.maximum(top, other_top)
            mass = st_ref[row, GROUPS:] * jnp.exp(top - both)
            other_mass = pst_ref[row, GROUPS:] * jnp.exp(other_top - both)
            everything = mass + other_mass
            ld_ref[row, :GROUPS] = both + jnp.log(everything)
            inverse = 1.0 / everything
            for image in range(GROUPS):
                at = slice(image, image + 1)
                wide = (QUERIES, HEADS * QUERIES)
                shares.append(jnp.broadcast_to((mass * inverse)[at], wide))
                other_shares.append(jnp.broadcast_to((other_mass * inverse)[at], wide))
        own = own_query(tokens)

        def spread(parts):
            high, rest = two_terms(jnp.where(own, jnp.concatenate(parts, axis=0), 0.0))
            return nn(high, map_ref[...]) + nn(rest, map_ref[...])

        out_ref[...] = spread(shares) * o_ref[...].reshape(tokens, width).astype(F32) + spread(
            other_shares
        ) * po_ref[...].reshape(tokens, width).astype(F32)
        for row in range(rows):
            for group in range(GROUPS):
                to = row * length + group * QUERIES
                at = pl.multiple_of(row * length + order[row, group] * QUERIES, QUERIES)
                stack_ref[to : to + QUERIES, cas] = out_ref[pl.ds(at, QUERIES)].astype(BF16)
        residual = n_ref[...].reshape(tokens, width) * gain_ref[0:1] + shift_ref[0:1]
        normed, inverse = norm(residual + nn(stack_ref[:, cas], wx_ref[...]) + cb_ref[2:3])
        n2_ref[...] = normed
        inv2_ref[...] = inverse
        x2 = normed * gain_ref[1:2] + shift_ref[1:2]
        x2_ref[...] = x2
        stack_ref[:, zs] = x2.astype(BF16)

    @pl.when(phase == 0)
    def _():
        feed_forward_step(
            (stack_ref, slope_ref, sum_ref), step, stack_ref[:, zs], we_ref[...], be_ref[...],
            wr_ref[...],
        )

    @pl.when((phase == 1) & (step == 0))
    def _():
        normed, inverse = norm(x2_ref[...] + sum_ref[...] + br_ref[0:1])
        mixed = normed * gain_ref[2:3] + shift_ref[2:3]
        mixed_ref[...] = mixed.astype(BF16).reshape(rows, length, width)
        slopes = cot_ref[...].reshape(tokens, width).astype(F32)
        dh = norm_backward(slopes, normed, inverse, gain_ref[2:3])
        vec_ref[...] = jnp.zeros_like(vec_ref)
        vec_ref[0:1] = total(dh)
        vec_ref[1:2] = total(slopes * normed)
        vec_ref[2:3] = total(slopes)
        dh_ref[...] = dh
        stack_ref[:, dhs] = dh.astype(BF16)

    @pl.when(phase == 1)
    def _():
        feed_backward_step(
            stack_ref, be_slope_ref, slope_ref, sum_ref, steps - 1 - step, step == 0,
            stack_ref[:, dhs], we_ref[...], wr_ref[...], inner,
        )

    @pl.when((phase == 1) & (step == steps - 1))
    def _():
        dz = dh_ref[...] + sum_ref[...]
        normed = n2_ref[...]
        dh2 = norm_backward(dz, normed, inv2_ref[...], gain_ref[1:2])
        vec_ref[3:4] = total(dz * normed)
        vec_ref[4:5] = total(dz)
        vec_ref[5:6] = total(dh2)
        dh2_ref[...] = dh2.reshape(rows, length, width)
        low = dh2.astype(BF16)
        stack_ref[:, dh2s] = low
        dca = nt(low, wx_ref[...]).astype(BF16)
        for row in range(rows):
            for group in range(GROUPS):
                at = row * length + group * QUERIES
                to = pl.multiple_of(order[row, group] * QUERIES, QUERIES)
                dca_ref[row, pl.ds(to, QUERIES)] = dca[at : at + QUERIES]
        high, rest = two_terms(
            dca_ref[...].reshape(tokens, width).astype(F32) * out_ref[...]
        )
        delta = jnp.where(own_query(tokens), nt(high, map_ref[...]) + nt(rest, map_ref[...]), 0.0)
        for row in range(rows):
            for image in range(GROUPS):
                at = row * length + image * QUERIES
                ld_ref[row, GROUPS + image : GROUPS + image + 1] = total(delta[at : at + QUERIES])


def query_branch(
    order, o, po, st, pst, n1, cot, we, be, wr, br, gain, shift, wx, cb, mixed
):
    rows, sequence, width = n1.shape
    inner = we.shape[1] // 2
    steps = inner // CHUNK
    length = GROUPS * QUERIES
    tokens = rows * length
    half = pl.BlockSpec((rows, length, width), lambda *_: (0, 0, 0))
    wide = 2 * inner + 4 * width
    lanes = HEADS * QUERIES
    return pl.pallas_call(
        query_kernel,
        grid_spec=pltpu.PrefetchScalarGridSpec(
            num_scalar_prefetch=1,
            grid=(2, steps),
            in_specs=[whole(a.shape) for a in (o, po, st, pst)]
            + [half, half]
            + branch_specs(0, steps, width)
            + [whole(a.shape) for a in (br, gain, shift, wx, cb)]
            + [pl.BlockSpec(memory_space=pl.ANY)],
            out_specs=[
                half,
                whole((tokens, wide)),
                whole((rows, length, width)),
                whole((rows, length, width)),
                whole((rows, 2 * GROUPS, lanes)),
                whole((1, inner)),
                whole((8, width)),
            ],
            scratch_shapes=[
                pltpu.VMEM((steps, tokens, CHUNK), F32),
                pltpu.VMEM((tokens, width), F32),
                pltpu.VMEM((tokens, width), F32),
                pltpu.VMEM((tokens, width), F32),
                pltpu.VMEM((tokens, width), F32),
                pltpu.VMEM((tokens, width), F32),
                pltpu.VMEM((tokens, 1), F32),
                pltpu.VMEM((lanes, width), BF16),
            ],
        ),
        out_shape=[
            jax.ShapeDtypeStruct((rows, sequence, width), BF16),
            jax.ShapeDtypeStruct((tokens, wide), BF16),
            jax.ShapeDtypeStruct((rows, length, width), F32),
            jax.ShapeDtypeStruct((rows, length, width), BF16),
            jax.ShapeDtypeStruct((rows, 2 * GROUPS, lanes), F32),
            jax.ShapeDtypeStruct((1, inner), F32),
            jax.ShapeDtypeStruct((8, width), F32),
        ],
        input_output_aliases={15: 0},
        compiler_params=params(2),
        cost_estimate=pl.CostEstimate(
            flops=18 * tokens * width * inner, bytes_accessed=2 * 10**7, transcendentals=0
        ),
        name="query_branch",
    )(order, o, po, st, pst, n1, cot, we, be, wr, br, gain, shift, wx, cb, mixed)


def self_backward_kernel(
    lengths, order, dcq_ref, pdcq_ref, dh2_ref, dz_ref, n_ref, inv_ref, qkv_ref, lse_ref,
    ws_ref, wo_ref, wq_ref, gain_ref,
    grad_ref, dqkv_ref, low_ref, dcq_low_ref, vec_ref, dcq_sum, dx_ref, datt_ref, bias_ref,
):
    row = pl.program_id(0)
    sequence, width = n_ref.shape[1:]
    length = GROUPS * QUERIES

    @pl.when(row == 0)
    def _():
        vec_ref[...] = jnp.zeros_like(vec_ref)

    bias_ref[...] = same_group(lengths, row, sequence)
    dcq = dcq_ref[0].astype(F32) + pdcq_ref[0].astype(F32)
    dcq_sum[...] = dcq
    vec_ref[0:1] += total(dcq)
    for group in range(GROUPS):
        at = pl.multiple_of(order[row, group] * QUERIES, QUERIES)
        dcq_low_ref[0, group * QUERIES : (group + 1) * QUERIES] = dcq_sum[
            pl.ds(at, QUERIES)
        ].astype(BF16)
    dx_ref[:length] = dh2_ref[0] + nt(dcq_low_ref[0], wq_ref[...])
    dx_ref[length:] = dz_ref[0]
    dx, normed = dx_ref[...], n_ref[0]
    vec_ref[1:2] += total(dx * normed)
    vec_ref[2:3] += total(dx)
    dh = norm_backward(dx, normed, inv_ref[0], gain_ref[0:1])
    vec_ref[3:4] += total(dh)
    dx_ref[...] = dh
    low_ref[0] = dh.astype(BF16)
    datt_ref[...] = nt(low_ref[0], wo_ref[...]).astype(BF16)
    scale = (width // HEADS) ** -0.5
    for part in range(width // WIDE):
        at = part * WIDE
        queries = qkv_ref[0, :, at : at + WIDE]
        keys = qkv_ref[0, :, width + at : width + at + WIDE]
        values = qkv_ref[0, :, 2 * width + at : 2 * width + at + WIDE]
        slopes = datt_ref[:, at : at + WIDE]
        dq = jnp.zeros((sequence, WIDE), F32)
        dk = jnp.zeros((sequence, WIDE), F32)
        dv = jnp.zeros((sequence, WIDE), F32)
        for head in range(4):
            own = only_head(queries, head)
            scores = nt(keys, own * jnp.asarray(scale, BF16)) + bias_ref[...]
            probs = jnp.exp(scores - lse_ref[0, 4 * part + head : 4 * part + head + 1])
            out_slopes = only_head(slopes, head)
            prob_slopes = nt(values, out_slopes)
            delta = total(probs * prob_slopes)
            low = (probs * (prob_slopes - delta) * scale).astype(BF16)
            dv += nn(probs.astype(BF16), out_slopes)
            dk += nn(low, own)
            dq += tn(low, only_head(keys, head))
        vec_ref[4:5, at : at + WIDE] += total(dq)
        vec_ref[5:6, at : at + WIDE] += total(dv)
        dqkv_ref[0, :, at : at + WIDE] = dq.astype(BF16)
        dqkv_ref[0, :, width + at : width + at + WIDE] = dk.astype(BF16)
        dqkv_ref[0, :, 2 * width + at : 2 * width + at + WIDE] = dv.astype(BF16)
    grad_ref[0] = (dx_ref[...] + nt(dqkv_ref[0], ws_ref[...])).astype(BF16)


def self_backward(lengths, order, dcq, pdcq, dh2, dz, n1, inv1, qkv, lse, ws, wo, wq, gain):
    rows, sequence, width = n1.shape
    length = GROUPS * QUERIES

    def by_row(*shape):
        return pl.BlockSpec((1, *shape), lambda r, *_: (r,) + (0,) * len(shape))

    def out(dtype, *shape):
        return jax.ShapeDtypeStruct((rows, *shape), dtype)

    return pl.pallas_call(
        self_backward_kernel,
        grid_spec=pltpu.PrefetchScalarGridSpec(
            num_scalar_prefetch=2,
            grid=(rows,),
            in_specs=[by_row(*a.shape[1:]) for a in (dcq, pdcq, dh2, dz, n1, inv1, qkv, lse)]
            + [whole(a.shape) for a in (ws, wo, wq, gain)],
            out_specs=[
                by_row(sequence, width),
                by_row(sequence, 3 * width),
                by_row(sequence, width),
                by_row(length, width),
                whole((8, width)),
            ],
            scratch_shapes=[
                pltpu.VMEM((length, width), F32),
                pltpu.VMEM((sequence, width), F32),
                pltpu.VMEM((sequence, width), BF16),
                pltpu.VMEM((sequence, sequence), F32),
            ],
        ),
        out_shape=[
            out(BF16, sequence, width),
            out(BF16, sequence, 3 * width),
            out(BF16, sequence, width),
            out(BF16, length, width),
            jax.ShapeDtypeStruct((8, width), F32),
        ],
        compiler_params=params(1),
        cost_estimate=pl.CostEstimate(
            flops=2 * rows * sequence * width * 9 * width, bytes_accessed=10**7, transcendentals=0
        ),
        name="self_backward",
    )(lengths, order, dcq, pdcq, dh2, dz, n1, inv1, qkv, lse, ws, wo, wq, gain)


def local(
    sizes,
    hidden,
    lengths,
    image_order,
    features,
    cotangent,
    self_weight,
    output_weight,
    self_bias,
    norm_gain,
    norm_shift,
    query_weight,
    image_weight,
    cross_weight,
    cross_bias,
    expand_weight,
    expand_bias,
    reduce_weight,
    reduce_bias,
):
    row_count, sequence, width = hidden.shape
    inner = reduce_weight.shape[0] // 2
    local_count = features.shape[2]
    slots = -(-local_count // 16) * 16
    length = GROUPS * QUERIES
    patch = lax.axis_index("patch").astype(jnp.int32)
    pair = sizes["patch"] == 2

    qkv, attended, lse, n1, inv1, low1, cq = self_forward(
        lengths, image_order, hidden, self_weight, output_weight, query_weight,
        self_bias, norm_gain, norm_shift, cross_bias,
    )

    def swap(array):
        return lax.ppermute(array, "patch", [(0, 1), (1, 0)])

    if pair:
        other_cq = swap(cq)
    else:
        other_cq = lax.all_gather(cq, "patch", axis=0, tiled=True)
    mixed, text_stack, dz_text, be_text, vec_text = text_branch(
        n1, low1, cotangent, expand_weight, expand_bias.reshape(1, -1), reduce_weight, reduce_bias,
        norm_gain, norm_shift,
    )
    kv = image_forward(features, image_weight, cross_bias, slots)
    if pair:
        here = jnp.stack([patch * row_count, patch])
        there = jnp.stack([(1 - patch) * row_count, patch])
        for_other, for_other_st = cross_forward(there, kv, other_cq, slots, local_count)
        po, pst = swap(for_other), swap(for_other_st)
        o, st = cross_forward(here, kv, cq, slots, local_count)
    else:
        here = jnp.stack([jnp.zeros_like(patch), patch])
        every_o, every_st = cross_forward(here, kv, other_cq, slots, local_count)
        top, mass = every_st[:, :GROUPS], every_st[:, GROUPS:]
        both = lax.pmax(top, "patch")
        mass = mass * jnp.exp(top - both)
        everything = lax.psum(mass, "patch")
        share = (mass / everything).reshape(-1, GROUPS, HEADS, QUERIES).transpose(0, 1, 3, 2)
        every_o = every_o.reshape(-1, GROUPS, QUERIES, HEADS, width // HEADS) * share[..., None]
        o = lax.psum_scatter(
            every_o.astype(BF16).reshape(-1, length, width), "patch", scatter_dimension=0, tiled=True
        )
        st = lax.dynamic_slice_in_dim(
            jnp.concatenate([both, everything], axis=1), patch * row_count, row_count, 0
        )
        po = jnp.zeros_like(o)
        pst = jnp.concatenate([st[:, :GROUPS], jnp.zeros_like(st[:, GROUPS:])], axis=1)
    mixed, query_stack, dh2, dca, ld, be_query, vec_query = query_branch(
        image_order, o, po, st, pst, n1, cotangent, expand_weight, expand_bias.reshape(1, -1),
        reduce_weight, reduce_bias, norm_gain, norm_shift, cross_weight, cross_bias, mixed,
    )
    if pair:
        other_dca, other_ld = swap(dca), swap(ld)
        dcq, dkv, dcv_sum = cross_backward(here, kv, cq, dca, ld, slots, local_count)
        for_other, other_dkv, other_sum = cross_backward(
            there, kv, other_cq, other_dca, other_ld, slots, local_count
        )
        pdcq = swap(for_other)
        dcv_sum = dcv_sum + other_sum
        own_first = patch == 0
        dkv = jnp.concatenate(
            [jnp.where(own_first, dkv, other_dkv), jnp.where(own_first, other_dkv, dkv)], axis=0
        )
    else:
        every_dca = lax.all_gather(dca, "patch", axis=0, tiled=True)
        every_ld = lax.all_gather(ld, "patch", axis=0, tiled=True)
        every_dcq, dkv, dcv_sum = cross_backward(
            here, kv, other_cq, every_dca, every_ld, slots, local_count
        )
        dcq = lax.psum_scatter(every_dcq, "patch", scatter_dimension=0, tiled=True)
        pdcq = jnp.zeros_like(dcq)
    grad, dqkv, dh1, dcq_low, vec_self = self_backward(
        lengths, image_order, dcq, pdcq, dh2, dz_text, n1, inv1, qkv, lse,
        self_weight, output_weight, query_weight, norm_gain,
    )

    def cut(stack, at, wide):
        return stack[:, at : at + wide]

    def flat(array):
        return array.reshape(-1, array.shape[-1])

    dkv_used = dkv.reshape(-1, slots, 2 * width)[:, :local_count].reshape(-1, 2 * width)
    gradients = [
        tn(flat(hidden), flat(dqkv)),
        tn(flat(attended), flat(dh1)),
        tn(flat(low1[:, :length]), flat(dcq_low)),
        tn(flat(features), dkv_used),
        tn(cut(query_stack, 2 * inner + 2 * width, width), cut(query_stack, 2 * inner + 3 * width, width)),
        jnp.concatenate(
            [tn(cut(s, 2 * inner, width), cut(s, inner, inner)) for s in (query_stack, text_stack)],
            axis=1,
        ),
        jnp.concatenate(
            [tn(cut(s, 0, inner), cut(s, 2 * inner + width, width)) for s in (query_stack, text_stack)],
            axis=0,
        ),
    ]

    def scatter(array):
        array = lax.psum_scatter(array.astype(BF16), "dp", scatter_dimension=0, tiled=True)
        array = lax.psum_scatter(array, "patch", scatter_dimension=1, tiled=True)
        return array.astype(F32)

    summed = [scatter(g) for g in gradients]
    vectors = lax.psum(
        (
            jnp.concatenate([vec_self[4:5], vec_self[5:6], vec_self[3:4]]),
            jnp.concatenate([vec_self[1:2], vec_query[3:4], vec_query[1:2], vec_text[1:2]]),
            jnp.concatenate([vec_self[2:3], vec_query[4:5], vec_query[2:3], vec_text[2:3]]),
            jnp.concatenate([vec_self[0:1], dcv_sum, vec_query[5:6]]),
            jnp.concatenate([be_query[0], be_text[0]]),
            jnp.concatenate([vec_query[0:1], vec_text[0:1]]),
        ),
        ("dp", "patch"),
    )
    return (
        mixed,
        grad,
        summed[0],
        summed[1],
        vectors[0],
        vectors[1],
        vectors[2],
        summed[2],
        summed[3],
        summed[4],
        vectors[3],
        summed[5],
        vectors[4],
        summed[6],
        vectors[5],
    )


def solution(mesh):
    rows = P(("dp", "patch"), None, None)
    counts = P(("dp", "patch"), None)
    matrix = P("dp", "patch")
    return jax.shard_map(
        functools.partial(local, dict(mesh.shape)),
        mesh=mesh,
        in_specs=(rows, counts, counts, P("dp", None, "patch", None), rows) + (P(),) * 13,
        out_specs=(
            rows, rows, matrix, matrix, P(), P(), P(), matrix, matrix, matrix, P(), matrix, P(),
            matrix, P(),
        ),
        check_vma=False,
    )
```

time: 1160 us -> 823 us (0.71); the launches traced: 1140 us -> 819 us
  matrix products: 201 us -> 37.7 us
  local copies, waits for them, and re-layouts: 229 us -> 67.8 us
  Pallas kernels: 0 us -> 127 us
  blocking collectives: 49.7 us -> 0 us
  other arithmetic: 84 us -> 38.9 us
  waiting for transfers between devices: 564 us -> 525 us
    dot_general x42 -> x9, matrix products: 201 us -> 37.7 us  [tn(): lax.dot_general(left, right, (((0,), (0,)), ((), ())), preferred_element_...]
    pallas_call x0 -> x9, Pallas kernels: none -> 127 us  [the longest x1 32.5 us: query_branch(): pl.pallas_call(query_kernel, grid_spec=pltpu.PrefetchScalarGridSpec(num_s...]
    psum x1, waiting for transfers between devices: 131 us -> 22.2 us  [local(): lax.psum((jnp.concatenate([vec_self[4:5], vec_self[5:6], vec_self[3:4]]),...]
    convert_element_type x13 -> x0, local copies, waits for them, and re-layouts: 43.5 us -> none  [the longest x1 21.2 us: score_slopes(): paired = jnp.stack([key_slope, value_slope], axis=3).astype(jnp.bfloat16)]
    unnamed x202 -> x57, local copies, waits for them, and re-layouts: 84.6 us -> 44.2 us
    reduce_scatter x10 -> x8, waiting for transfers between devices: 262 us -> 301 us  [the longest x5 256 us: scatter(): lax.psum_scatter(array.astype(BF16), 'dp', scatter_dimension=0, tiled=True)]
    reshape x6 -> x2, local copies, waits for them, and re-layouts: 46.4 us -> 16.5 us  [the longest x1 8.4 us: local(): dkv.reshape(-1, slots, 2 * width)[:, :local_count].reshape(-1, 2 * width)]
    another operation x18 -> x0, local copies, waits for them, and re-layouts: 25.2 us -> none  [the longest x2 13 us: score_slopes(): paired = jnp.stack([key_slope, value_slope], axis=3).astype(jnp.bfloat16)]
  transfers between devices with their start and end apart: 17 -> 21, of which waited for: 12 -> 15; matrix products, arithmetic and copies ran while one was open for 24% -> 16% of each run, Pallas kernels for 0% -> 9%
where the time goes in v1:
time: 823 us; the launch traced here: 819 us
  waiting for transfers between devices  525 us (64%)
  Pallas kernels  127 us (15%)
  local copies, waits for them, and re-layouts  67.8 us (8%)
  other arithmetic  38.9 us (5%)
  matrix products  37.7 us (5%)
  between operations  15.9 us (2%)
    reduce_scatter x5, waiting for transfers between devices, scatter(): lax.psum_scatter(array.astype(BF16), 'dp', scatter_dimension=0, tiled=True)  256 us
    unnamed x21, waiting for transfers between devices  193 us
    reduce_scatter x3, waiting for transfers between devices, scatter(): array = lax.psum_scatter(array, 'patch', scatter_dimension=1, tiled=True)  45.7 us
    unnamed x57, local copies, waits for them, and re-layouts  44.2 us
    dot_general x9, matrix products, tn(): lax.dot_general(left, right, (((0,), (0,)), ((), ())), preferred_element_...  37.7 us
    pallas_call x1, Pallas kernels, query_branch(): pl.pallas_call(query_kernel, grid_spec=pltpu.PrefetchScalarGridSpec(num_s...  32.5 us
    psum x1, waiting for transfers between devices, local(): lax.psum((jnp.concatenate([vec_self[4:5], vec_self[5:6], vec_self[3:4]]),...  22.2 us
    pallas_call x2, Pallas kernels, cross_backward(): pl.pallas_call(functools.partial(cross_backward_kernel, slots, local_coun...  20.3 us
  transfers between devices with their start and end apart: 21, of which 15 were waited for; matrix products, arithmetic and copies ran while one was open for 16% of the time, Pallas kernels for 9%

profile of v1, /device:TPU:8, one launch (start us, length us, event | category | flops | bytes accessed | tf_op | source)
XLA Modules:
  0.0 819.1 jit_solution(13586505563751550564)
XLA Ops:
  8.1 12.1 %self_forward.1 = (bf16[2,256,2304]{2,1,0:T(8,128)(2,1)}, bf16[2,256,768]{2,1,0:T(8,128)(2,1)}, f32[2,12,256]{2,1,0:T(8,128)}, f32[2,256,768]{2,1,0:T(8,128)}, f...) custom-call(s32[2,4]{1,0:T(2,128)} %lengths.3, s32[2,4]{1,0:T(2,128)} %order.5, ...), custom_call_target="tpu_custom_call" | custom-call | flops 3019898880 | bytes 10000000 | tf_op jit(solution)/shard_map/self_forward/pallas_call | solution.py:143
  25.0 15.8 %image_forward.1.kv_ref = bf16[4,576,1536]{2,1,0:T(8,128)(2,1)} custom-call(bf16[4,4,132,1408]{3,2,1,0:T(8,128)(2,1)} %copy.47.x_ref, bf16[1408,1536]{1,0:T(8,128)(2,1)} %w_ref.1, f32[3,768]{1,0:T(4,128)} %cb_ref.5), custom_call_target="tpu_custom_call" | custom-call | flops 9965666304 | bytes 10000000 | tf_op jit(solution)/shard_map/image_forward/pallas_call | solution.py:195
  40.8 15.6 %text_branch.1 = (bf16[2,256,768]{2,1,0:T(8,128)(2,1)}, bf16[256,7680]{1,0:T(8,128)(2,1)}, f32[2,128,768]{2,1,0:T(8,128)}, f32[1,3072]{1,0:T(1,128)}, f32[8,768]{1,0:T(8,128)}) custom-call(f32[2,256,768]{2,1,0:T(8,128)} %get-tuple-element.54.n_ref, bf16[2,256,768]{2,1,0:T(8,128)(2,1)} %get-tuple-element.55.low_ref, bf16[2,256,768]{2,1,0:T(8,128)(2,1)} %cot_ref.3, ...), custom_call_target="tpu_custom_call" | custom-call | flops 9663676416 | bytes 20000000 | tf_op jit(solution)/shard_map/text_branch/pallas_call | solution.py:454
  75.8 32.5 %query_branch.1 = (bf16[2,256,768]{2,1,0:T(8,128)(2,1)}, bf16[256,9216]{1,0:T(8,128)(2,1)}, f32[2,128,768]{2,1,0:T(8,128)}, bf16[2,128,768]{2,1,0:T(8,128)(2,1)}...) custom-call(s32[2,4]{1,0:T(2,128)} %order.5, ...), custom_call_target="tpu_custom_call", output_to_operand_aliasing={{0}: (15, {})} | custom-call | flops 10871635968 | bytes 20000000 | tf_op jit(solution)/shard_map/query_branch/pallas_call | solution.py:623
  120.2 10.2 %cross_backward.3 = (bf16[2,128,768]{2,1,0:T(8,128)(2,1)}, bf16[2,576,1536]{2,1,0:T(8,128)(2,1)}, f32[1,768]{1,0:T(1,128)}) custom-call(s32[2]{0:T(128)} %pad_add_fusion.1.place, bf16[4,576,1536]{2,1,0:T(8,128)(2,1)} %image_forward.1.kv_ref, bf16[2,128,768]{2,1,0:T(8,128)(2,1)} %copy-done.9, bf16[2,128,768]{2,1,0:T(8,128)(2,1)} %copy-done.11, ...), custom_call_target="tpu_custom_call" | custom-call | flops 8000000000 | bytes 8000000 | tf_op jit(solution)/shard_map/cross_backward/pallas_call | solution.py:326
  130.9 10.2 %cross_backward.2 = (bf16[2,128,768]{2,1,0:T(8,128)(2,1)}, bf16[2,576,1536]{2,1,0:T(8,128)(2,1)}, f32[1,768]{1,0:T(1,128)}) custom-call(s32[2]{0:T(128)} %pad_add_fusion.place, bf16[4,576,1536]{2,1,0:T(8,128)(2,1)} %image_forward.1.kv_ref, bf16[2,128,768]{2,1,0:T(8,128)(2,1)} %get-tuple-element.49.q_ref, bf16[2,128,768]{2,1,0:T(8,128)(2,1)} %get-tuple-element.58.do_ref, ...), custom_call_target="tpu_custom_call" | custom-call | flops 8000000000 | bytes 8000000 | tf_op jit(solution)/shard_map/cross_backward/pallas_call | solution.py:326
  141.8 18.5 %self_backward.1 = (bf16[2,256,768]{2,1,0:T(8,128)(2,1)}, bf16[2,256,2304]{2,1,0:T(8,128)(2,1)}, bf16[2,256,768]{2,1,0:T(8,128)(2,1)}, bf16[2,128,768]{2,1,0:T(8,128)(2,1)}, f32[8,768]{1,0:T(8,128)}) custom-call(s32[2,4]{1,0:T(2,128)} %lengths.3, s32[2,4]{1,0:T(2,128)} %order.5, bf16[2,128,768]{2,1,0:T(8,128)(2,1)} %get-tuple-element.60.dcq_ref, ...), custom_call_target="tpu_custom_call" | custom-call | flops 5435817984 | bytes 10000000 | tf_op jit(solution)/shard_map/self_backward/pallas_call | solution.py:742
  173.6 8.1 reshape.52
  199.0 8.4 %reshape.22 = bf16[2112,1536]{1,0:T(8,128)(2,1)} reshape(bf16[16,132,1536]{2,1,0:T(8,128)(2,1)} %slice.106) | data formatting | bytes 12976128 | tf_op jit(solution)/shard_map/reshape | solution.py:882
  207.4 16.1 %fusion = bf16[1408,1536]{0,1:T(8,128)(2,1)} fusion(bf16[2112,1536]{1,0:T(8,128)(2,1)} %reshape.22, bf16[2112,1408]{1,0:T(8,128)(2,1)} %reshape.52), kind=kOutput, calls=%fused_computation.5 | convolution fusion | flops 9137356800 | bytes 16760832 | tf_op jit(solution)/shard_map/dot_general | solution.py:36
  235.0 15.4 %pad_maximum_fusion.1 = bf16[6144,768]{1,0:T(8,128)(2,1)} fusion(bf16[3072,768]{1,0:T(8,128)(2,1)S(1)} %convolution_convert_fusion.1, bf16[3072,768]{1,0:T(8,128)(2,1)S(1)} %convolution_convert_fusion.2), kind=kLoop, calls=%fused_computation.1 | loop fusion | flops 18874368 | bytes 18874368 | tf_op jit(solution)/shard_map/concatenate | solution.py:893
  264.3 28.7 %reduce-scatter.31.cloned.1.call-done = bf16[48,768]{1,0:T(8,128)(2,1)} async-done(((bf16[768,768]{1,0:T(8,128)(2,1)}), bf16[48,768]{1,0:T(8,128)(2,1)}) %reduce-scatter.31.cloned.1.call-update) | async-done | bytes 73744 | tf_op jit(solution)/shard_map/reduce_scatter | solution.py:900
  294.8 68.6 %reduce-scatter.43.cloned.1.call-done = bf16[48,2304]{1,0:T(8,128)(2,1)} async-done(((bf16[768,2304]{1,0:T(8,128)(2,1)}), bf16[48,2304]{1,0:T(8,128)(2,1)}) %reduce-scatter.43.cloned.1.call-update) | async-done | bytes 221200
  365.4 73.6 %reduce-scatter.49.cloned.1.call-done = bf16[88,1536]{1,0:T(8,128)(2,1)} async-done(((bf16[1408,1536]{1,0:T(8,128)(2,1)}), bf16[88,1536]{1,0:T(8,128)(2,1)}) %reduce-scatter.49.cloned.1.call-update) | async-done | bytes 270352
  441.0 113.4 %reduce-scatter.41.cloned.1.call-done = bf16[384,768]{1,0:T(8,128)(2,1)} async-done(((bf16[6144,768]{1,0:T(8,128)(2,1)}), bf16[384,768]{1,0:T(8,128)(2,1)}) %reduce-scatter.41.cloned.1.call-update) | async-done | bytes 589840 | tf_op jit(solution)/shard_map/reduce_scatter | solution.py:900
  556.6 113.6 %reduce-scatter.37.cloned.1.call-done = bf16[48,6144]{1,0:T(8,128)(2,1)} async-done(((bf16[768,6144]{1,0:T(8,128)(2,1)}), bf16[48,6144]{1,0:T(8,128)(2,1)}) %reduce-scatter.37.cloned.1.call-update) | async-done | bytes 589840 | tf_op jit(solution)/shard_map/reduce_scatter | solution.py:900
  673.7 9.3 %reduce-scatter.51.cloned.1.call-done = bf16[384,48]{1,0:T(8,128)(2,1)} async-done(((bf16[768,48]{1,0:T(8,128)(2,1)}), bf16[384,48]{1,0:T(8,128)(2,1)}) %reduce-scatter.51.cloned.1.call-update) | async-done | bytes 36880
  684.7 12.2 %reduce-scatter.45.cloned.1.call-done = bf16[384,48]{1,0:T(8,128)(2,1)} async-done(((bf16[768,48]{1,0:T(8,128)(2,1)}), bf16[384,48]{1,0:T(8,128)(2,1)}) %reduce-scatter.45.cloned.1.call-update) | async-done | bytes 36880
  698.5 12.0 %reduce-scatter.47.cloned.1.call-done = bf16[384,48]{1,0:T(8,128)(2,1)} async-done(((bf16[768,48]{1,0:T(8,128)(2,1)}), bf16[384,48]{1,0:T(8,128)(2,1)}) %reduce-scatter.47.cloned.1.call-update) | async-done | bytes 36880
  712.2 16.6 %reduce-scatter.27.cloned.1.call-done = bf16[48,1152]{0,1:T(8,128)(2,1)} async-done(((bf16[48,2304]{0,1:T(8,128)(2,1)}), bf16[48,1152]{0,1:T(8,128)(2,1)}) %reduce-scatter.27.cloned.1.call-update) | async-done | bytes 110608 | tf_op jit(solution)/shard_map/reduce_scatter | solution.py:901
  730.6 13.6 %reduce-scatter.33.cloned.1.call-done = bf16[88,768]{0,1:T(8,128)(2,1)} async-done(((bf16[88,1536]{0,1:T(8,128)(2,1)}), bf16[88,768]{0,1:T(8,128)(2,1)}) %reduce-scatter.33.cloned.1.call-update) | async-done | bytes 135184 | tf_op jit(solution)/shard_map/reduce_scatter | solution.py:901
  745.9 16.5 %reduce-scatter.53.cloned.1.call-done = bf16[384,384]{1,0:T(8,128)(2,1)} async-done(((bf16[768,384]{1,0:T(8,128)(2,1)}), bf16[384,384]{1,0:T(8,128)(2,1)}) %reduce-scatter.53.cloned.1.call-update) | async-done | bytes 294928
  764.4 15.5 %reduce-scatter.39.cloned.1.call-done = bf16[48,3072]{1,0:T(8,128)(2,1)} async-done(((bf16[48,6144]{1,0:T(8,128)(2,1)}), bf16[48,3072]{1,0:T(8,128)(2,1)}) %reduce-scatter.39.cloned.1.call-update) | async-done | bytes 294928 | tf_op jit(solution)/shard_map/reduce_scatter | solution.py:901
  781.7 22.2 %all-reduce.3.cloned.1.call-done = (f32[3,768]{1,0:T(4,128)}, f32[4,768]{1,0:T(4,128)}, f32[4,768]{1,0:T(4,128)}, f32[3,768]{1,0:T(4,128)}, f32[6144]{0:T(1024)}, /*index=5*/f32[2,768]{1,0:T(2,128)}) async-done(((f32[3,768]{1,0:T(4,128)}, f32[4,768]{1,0:T(4,128)}, f32[4,768]{1,0:T(4,128)}, f32[3,768]{1,0:T(4,128)}, f32[6144]{0:T(1024)}, /*index=5*/f32[2,768]{1,0:T(2,128)}), (f32[3,768]{1,0:T(4,128)}, ...) | async-done | bytes 73744 | tf_op jit(solution)/shard_map/psum | solution.py:905
  (132 shorter events, 124.5 us)
Async XLA Ops:
  8.0 252.7 %reduce-scatter.35.cloned.1.call-start = ((), (), s32[]{:S(2)}) async-start(), calls=%async_computation.18 | async-start | bytes 1253376 | tf_op jit(solution)/shard_map/reduce_scatter | solution.py:900
  20.2 36.8 %collective-permute-start = (bf16[2,128,768]{2,1,0:T(8,128)(2,1)}, bf16[2,128,768]{2,1,0:T(8,128)(2,1)S(1)}, u32[]{:S(2)}, u32[]{:S(2)}) collective-permute-start(bf16[2,128,768]{2,1,0:T(8,128)(2,1)} %get-tuple-element.49.q_ref), channel_id=1, source_target_pairs={{0,1},{1,0},{2,3},{3,2},{4,5},{5,4},{6,7},{7,6},{8,9},{9,8},{10,11... | collective-permute-start | bytes 1179656 | tf_op jit(solution)/shard_map/ppermute | solution.py:813
  63.8 11.3 %collective-permute-start.1 = (bf16[2,128,768]{2,1,0:T(8,128)(2,1)}, bf16[2,128,768]{2,1,0:T(8,128)(2,1)S(1)}, u32[]{:S(2)}, u32[]{:S(2)}) collective-permute-start(bf16[2,128,768]{2,1,0:T(8,128)(2,1)} %get-tuple-element.51), channel_id=1, source_target_pairs={{0,1},{1,0},{2,3},{3,2},{4,5},{5,4},{6,7},{7,6},{8,9},{9,8},{10,11... | collective-permute-start | bytes 1179656 | tf_op jit(solution)/shard_map/ppermute | solution.py:813
  64.9 10.2 %collective-permute-start.2 = (f32[2,8,384]{2,1,0:T(8,128)}, f32[2,8,384]{2,1,0:T(8,128)S(1)}, u32[]{:S(2)}, u32[]{:S(2)}) collective-permute-start(f32[2,8,384]{2,1,0:T(8,128)} %get-tuple-element.53), channel_id=1, source_target_pairs={{0,1},{1,0},{2,3},{3,2},{4,5},{5,4},{6,7},{7,6},{8,9},{9,8},{10,11... | collective-permute-start | bytes 73736 | tf_op jit(solution)/shard_map/ppermute | solution.py:813
  108.4 10.4 %collective-permute-start.3 = (bf16[2,128,768]{2,1,0:T(8,128)(2,1)}, bf16[2,128,768]{2,1,0:T(8,128)(2,1)S(1)}, u32[]{:S(2)}, u32[]{:S(2)}) collective-permute-start(bf16[2,128,768]{2,1,0:T(8,128)(2,1)} %get-tuple-element.58.do_ref), channel_id=1, source_target_pairs={{0,1},{1,0},{2,3},{3,2},{4,5},{5,4},{6,7},{7,6},{8,9},{9,8},{10,11... | collective-permute-start | bytes 1179656 | tf_op jit(solution)/shard_map/ppermute | solution.py:813
  109.0 9.8 %collective-permute-start.4 = (f32[2,8,384]{2,1,0:T(8,128)}, f32[2,8,384]{2,1,0:T(8,128)S(1)}, u32[]{:S(2)}, u32[]{:S(2)}) collective-permute-start(f32[2,8,384]{2,1,0:T(8,128)} %get-tuple-element.59.ld_ref), channel_id=1, source_target_pairs={{0,1},{1,0},{2,3},{3,2},{4,5},{5,4},{6,7},{7,6},{8,9},{9,8},{10,11... | collective-permute-start | bytes 73736 | tf_op jit(solution)/shard_map/ppermute | solution.py:813
  113.1 149.4 %reduce-scatter.29.cloned.1.call-start = ((), (), s32[]{:S(2)}) async-start(), calls=%async_computation.15 | async-start | bytes 1253376 | tf_op jit(solution)/shard_map/reduce_scatter | solution.py:900
  130.3 10.8 %collective-permute-start.5 = (bf16[2,128,768]{2,1,0:T(8,128)(2,1)}, bf16[2,128,768]{2,1,0:T(8,128)(2,1)S(1)}, u32[]{:S(2)}, u32[]{:S(2)}) collective-permute-start(bf16[2,128,768]{2,1,0:T(8,128)(2,1)} %get-tuple-element.61), channel_id=1, source_target_pairs={{0,1},{1,0},{2,3},{3,2},{4,5},{5,4},{6,7},{7,6},{8,9},{9,8},{10,11... | collective-permute-start | bytes 1179656 | tf_op jit(solution)/shard_map/ppermute | solution.py:813
  163.4 129.6 %reduce-scatter.31.cloned.1.call-start = ((), (), s32[]{:S(2)}) async-start(), calls=%async_computation.16 | async-start | bytes 1253376 | tf_op jit(solution)/shard_map/reduce_scatter | solution.py:900
  165.1 198.3 %reduce-scatter.43.cloned.1.call-start = ((), (), s32[]{:S(2)}) async-start(), calls=%async_computation.22 | async-start | bytes 3760128
  173.5 265.5 %reduce-scatter.49.cloned.1.call-start = ((), (), s32[]{:S(2)}) async-start(), calls=%async_computation.25 | async-start | bytes 4595712
  230.2 324.2 %reduce-scatter.41.cloned.1.call-start = ((), (), s32[]{:S(2)}) async-start(), calls=%async_computation.21 | async-start | bytes 10027008 | tf_op jit(solution)/shard_map/reduce_scatter | solution.py:900
  250.4 419.8 %reduce-scatter.37.cloned.1.call-start = ((), (), s32[]{:S(2)}) async-start(), calls=%async_computation.19 | async-start | bytes 10027008 | tf_op jit(solution)/shard_map/reduce_scatter | solution.py:900
  260.6 411.8 %copy-start.7 = (f32[1,768]{1,0:T(1,128)S(1)}, f32[1,768]{1,0:T(1,128)}, u32[]{:S(2)}) copy-start(f32[1,768]{1,0:T(1,128)} %get-tuple-element.79) | copy-start | bytes 9220
  260.6 411.8 %copy-start.8 = (f32[1,768]{1,0:T(1,128)S(1)}, f32[1,768]{1,0:T(1,128)}, u32[]{:S(2)}) copy-start(f32[1,768]{1,0:T(1,128)} %get-tuple-element.78) | copy-start | bytes 9220
  260.6 411.8 %copy-start.4 = (f32[8,768]{1,0:T(8,128)S(1)}, f32[8,768]{1,0:T(8,128)}, u32[]{:S(2)}) copy-start(f32[8,768]{1,0:T(8,128)} %get-tuple-element.71) | copy-start | bytes 73732
  260.6 422.4 %reduce-scatter.51.cloned.1.call-start = ((), (), s32[]{:S(2)}) async-start(), calls=%async_computation.26 | async-start | bytes 294912
  262.4 434.5 %reduce-scatter.45.cloned.1.call-start = ((), (), s32[]{:S(2)}) async-start(), calls=%async_computation.23 | async-start | bytes 294912
  264.2 446.4 %reduce-scatter.47.cloned.1.call-start = ((), (), s32[]{:S(2)}) async-start(), calls=%async_computation.24 | async-start | bytes 294912
  294.7 434.1 %reduce-scatter.27.cloned.1.call-start = ((), (), s32[]{:S(2)}) async-start(), calls=%async_computation.14 | async-start | bytes 884736 | tf_op jit(solution)/shard_map/reduce_scatter | solution.py:901
  365.4 378.8 %reduce-scatter.33.cloned.1.call-start = ((), (), s32[]{:S(2)}) async-start(), calls=%async_computation.17 | async-start | bytes 589824 | tf_op jit(solution)/shard_map/reduce_scatter | solution.py:901
  441.0 321.4 %reduce-scatter.53.cloned.1.call-start = ((), (), s32[]{:S(2)}) async-start(), calls=%async_computation.27 | async-start | bytes 884736
  556.6 223.3 %reduce-scatter.39.cloned.1.call-start = ((), (), s32[]{:S(2)}) async-start(), calls=%async_computation.20 | async-start | bytes 884736 | tf_op jit(solution)/shard_map/reduce_scatter | solution.py:901
  670.3 133.7 %all-reduce.3.cloned.1.call-start = ((), (), s32[]{:S(2)}) async-start(), calls=%async_computation.28 | async-start | bytes 159744 | tf_op jit(solution)/shard_map/psum | solution.py:905
  (15 other events, 1282.2 us)
Sparse Core Ops, SparseCore 0:
  113.2 58.2 reduce-scatter.34
  175.1 57.0 reduce-scatter.28
  235.9 57.0 reduce-scatter.30
  296.7 66.5 reduce-scatter.42
  367.0 71.9 reduce-scatter.48
  443.0 111.3 reduce-scatter.40
  559.1 111.0 reduce-scatter.36
  672.5 10.5 reduce-scatter.50
  685.9 11.0 reduce-scatter.44
  699.6 10.9 reduce-scatter.46
  713.4 15.3 reduce-scatter.26
  731.0 13.1 reduce-scatter.32
  747.0 15.3 reduce-scatter.52
  764.6 15.3 reduce-scatter.38
Sparse Core Ops, SparseCore 1:
  679.4 124.5 all-reduce.2
